TPU v7x, 32 devices: a whole 2x2x4 slice. The times are simulated.
32 devices in a mesh: parts: 2 (over x), tile: 8 (over z, y), stream: 2 (over core).
Axes of the slice: x: 2, y: 2, z: 4, core: 2. Of those that a mesh axis runs over, the one named last changes fastest.
Arguments:
- obs_rows: bfloat16 [131072, 128], P(('parts', 'tile', 'stream')), parts along dimension 0, may hold values from -6 to 6
- obs_instr: int32 [131072], P(('parts', 'tile', 'stream')), parts along dimension 0, may hold values from 0 to 3
- obs_target: int32 [131072, 1], P(('parts', 'tile', 'stream')), parts along dimension 0, may hold values from 0 to 15; in each aligned block of 4096 rows (0 to 4095, 4096 to 8191, ...) at most 512 rows name the same one
- obs_cell: int32 [131072], P(('parts', 'tile', 'stream')), parts along dimension 0, may hold values from 0 to 5759
- embed_weight: bfloat16 [8, 128, 256], P('stream'), may hold values from -0.5 to 0.5
- background: float32 [256], replicated, may hold values from -5 to 5
- stencil_taps: float32 [9, 256], replicated, may hold values from -2 to 2
- weight_in: bfloat16 [256, 1024], replicated, may hold values from -0.375 to 0.375
- weight_out: bfloat16 [1024, 256], replicated, may hold values from -0.1875 to 0.1875
- grid_cotangent: bfloat16 [128, 1440, 256], P(('parts', 'tile', 'stream')), parts along dimension 0, may hold values from -6 to 6
Outputs:
- grid_output: bfloat16 [128, 1440, 256], P(('parts', 'tile', 'stream')), parts along dimension 0
- embed_grad: float32 [16, 128, 256], P(('parts', 'stream')), parts along dimension 0
There are 2 independent parts, one for each index of `parts`. A program takes and returns all parts, laid end to end along the dimension named above; an argument that names none is the same for every part. Nothing has to cross between parts.
Inputs may be any that keep to these rules, and one draw needn't show every extreme that they name: `obs_target`: among the 4096 observations of one device at most 512 name the same target.
All inputs are finite; a program needn't handle non-finite values.
Results may differ from a plain program's by a relative error of at most 0.015.
Values may be sent and summed in bfloat16 or wider, within the bound.
A program may use at most 192 MiB of HBM per device.

v0:
```python
import functools

import jax
import jax.numpy as jnp
from jax import lax
from jax.experimental import pallas as pl
from jax.experimental.pallas import tpu as pltpu
from jax.sharding import PartitionSpec as P


def padded_2(block, sides, width):
    for axis, dim in sides:
        count = lax.axis_size(axis)
        forward = [(i, i + 1) for i in range(count - 1)]
        backward = [(target, source) for source, target in forward]
        low = lax.ppermute(
            lax.slice_in_dim(block, block.shape[dim] - width, None, axis=dim), axis, forward
        )
        high = lax.ppermute(lax.slice_in_dim(block, 0, width, axis=dim), axis, backward)
        block = jnp.concatenate([low, block, high], axis=dim)
    return block


def pack_kernel(slot_ref, code_ref, rows_ref, out_rows, out_codes, rows_wide, packed):
    rows = rows_ref.shape[0]
    slots = out_rows.shape[0]
    step = 256

    @pl.loop(0, rows // step)
    def _(block):
        at = pl.ds(pl.multiple_of(block * step, step), step)
        rows_wide[at, :] = rows_ref[at, :].astype(jnp.float32)

    @pl.loop(0, slots // step)
    def _(block):
        at = pl.ds(pl.multiple_of(block * step, step), step)
        packed[at, :] = jnp.zeros((step, packed.shape[1]), jnp.float32)

    group = 16

    @pl.loop(0, rows // group)
    def _(block):
        base = block * group
        for inner in range(group):
            slot = slot_ref[base + inner]
            packed[pl.ds(slot, 1), :] = rows_wide[pl.ds(base + inner, 1), :]
            out_codes[slot] = code_ref[base + inner]

    @pl.loop(0, slots // step)
    def _(block):
        at = pl.ds(pl.multiple_of(block * step, step), step)
        out_rows[at, :] = packed[at, :].astype(jnp.bfloat16)


def pack(slot_index, codes, rows, slot_total):
    count, features = rows.shape
    smem = pl.BlockSpec(memory_space=pltpu.SMEM)
    vmem = pl.BlockSpec(memory_space=pltpu.VMEM)
    return pl.pallas_call(
        pack_kernel,
        out_shape=(
            jax.ShapeDtypeStruct((slot_total, features), jnp.bfloat16),
            jax.ShapeDtypeStruct((slot_total,), jnp.int32),
        ),
        in_specs=[smem, smem, vmem],
        out_specs=(vmem, smem),
        scratch_shapes=[
            pltpu.VMEM((count, features), jnp.float32),
            pltpu.VMEM((slot_total, features), jnp.float32),
        ],
        compiler_params=pltpu.CompilerParams(vmem_limit_bytes=24 << 20),
    )(slot_index, codes, rows)


def deposit_kernel(
    instr_dev,
    capacity,
    code_ref,
    cell_ref,
    bound_ref,
    rows_ref,
    weight_ref,
    background_ref,
    sums_out,
    field_out,
    density_out,
    even_sums,
    odd_sums,
    even_count,
    odd_count,
    even_rows,
    odd_rows,
):
    cells = field_out.shape[0]
    features = rows_ref.shape[1]
    pairs = rows_ref.shape[0] // (2 * capacity)
    step = 480

    @pl.loop(0, instr_dev * cells // step)
    def _(block):
        at = pl.ds(pl.multiple_of(block * step, 32), step)
        even_sums[at, :] = jnp.zeros((step, features), jnp.float32)
        odd_sums[at, :] = jnp.zeros((step, features), jnp.float32)

    @pl.loop(0, cells // step)
    def _(block):
        at = pl.ds(pl.multiple_of(block * step, 32), step)
        even_count[at, :] = jnp.zeros((step, features), jnp.float32)
        odd_count[at, :] = jnp.zeros((step, features), jnp.float32)

    one = jnp.ones((1, features), jnp.float32)
    group = 8

    @pl.loop(0, pairs)
    def _(pair):
        first = pl.multiple_of(pair * 2 * capacity, capacity)
        second = pl.multiple_of(first + capacity, capacity)
        even_rows[...] = rows_ref[pl.ds(first, capacity), :].astype(jnp.float32)
        odd_rows[...] = rows_ref[pl.ds(second, capacity), :].astype(jnp.float32)

        @pl.loop(0, bound_ref[pair])
        def _(block):
            base = block * group
            for inner in range(group):
                place = base + inner
                even_code = code_ref[first + place]
                odd_code = code_ref[second + place]
                even_cell = cell_ref[first + place]
                odd_cell = cell_ref[second + place]
                even_sums[pl.ds(even_code, 1), :] += even_rows[pl.ds(place, 1), :]
                odd_sums[pl.ds(odd_code, 1), :] += odd_rows[pl.ds(place, 1), :]
                even_count[pl.ds(even_cell, 1), :] += one
                odd_count[pl.ds(odd_cell, 1), :] += one

    @pl.loop(0, cells // step)
    def _(block):
        start = pl.multiple_of(block * step, 32)
        at = pl.ds(start, step)
        pieces = []
        for sums in (even_sums, odd_sums):
            for number in range(instr_dev):
                piece = sums[pl.ds(number * cells + start, step), :]
                pieces.append(piece.astype(jnp.bfloat16))
        wide = jnp.concatenate(pieces, axis=1)
        sums_out[at, :] = wide
        deposit = jnp.dot(wide, weight_ref[...], preferred_element_type=jnp.float32)
        density = 1.0 + (even_count[at, :] + odd_count[at, :])
        density_out[at, :] = density
        density = jnp.concatenate([density] * (deposit.shape[1] // features), axis=1)
        field_out[at, :] = ((deposit + background_ref[...]) / density).astype(jnp.bfloat16)


def deposit_cells(codes, cells, bounds, rows, weights, background, instr_dev, band_cells, capacity):
    features = rows.shape[1]
    width = weights.shape[1]
    smem = pl.BlockSpec(memory_space=pltpu.SMEM)
    vmem = pl.BlockSpec(memory_space=pltpu.VMEM)
    sums = pltpu.VMEM((instr_dev * band_cells + 8, features), jnp.float32)
    counts = pltpu.VMEM((band_cells + 8, features), jnp.float32)
    held = pltpu.VMEM((capacity, features), jnp.float32)
    return pl.pallas_call(
        functools.partial(deposit_kernel, instr_dev, capacity),
        out_shape=(
            jax.ShapeDtypeStruct((band_cells, weights.shape[0]), jnp.bfloat16),
            jax.ShapeDtypeStruct((band_cells, width), jnp.bfloat16),
            jax.ShapeDtypeStruct((band_cells, features), jnp.float32),
        ),
        in_specs=[smem, smem, smem, vmem, vmem, vmem],
        out_specs=(vmem, vmem, vmem),
        scratch_shapes=[sums, sums, counts, counts, held, held],
        compiler_params=pltpu.CompilerParams(vmem_limit_bytes=58 << 20),
    )(codes, cells, bounds, rows, weights, background.reshape(1, width))


def sum_over_tile(value):
    count = lax.axis_size("tile")
    if count & (count - 1):
        return lax.psum(value.astype(jnp.bfloat16), "tile").astype(jnp.float32)
    distance = 1
    while distance < count:
        mine = value.astype(jnp.bfloat16)
        other = lax.ppermute(mine, "tile", [(i, i ^ distance) for i in range(count)])
        value = mine.astype(jnp.float32) + other.astype(jnp.float32)
        distance *= 2
    return value


def stencil(padded, stencil_taps, orient):
    row_count = padded.shape[0] - 2
    field = padded.astype(jnp.float32)
    summed = jnp.zeros((row_count,) + padded.shape[1:], jnp.float32)
    for row_step in range(3):
        for col_step in range(3):
            offset = 1 + orient * (row_step - 1)
            window = lax.slice_in_dim(field, offset, offset + row_count, axis=0)
            window = jnp.roll(window, -orient * (col_step - 1), axis=1)
            summed = summed + stencil_taps[row_step * 3 + col_step] * window
    return summed


def branch(mixed, weight_in, weight_out):
    inverse_rms = lax.rsqrt(jnp.mean(mixed * mixed, axis=-1, keepdims=True) + 1e-06)
    normed = (mixed * inverse_rms).astype(jnp.bfloat16)
    hidden = jax.nn.gelu(
        jnp.dot(normed, weight_in, preferred_element_type=jnp.float32), approximate=True
    ).astype(jnp.bfloat16)
    return jnp.dot(hidden, weight_out, preferred_element_type=jnp.float32)


def on_device(
    obs_rows,
    obs_instr,
    obs_target,
    obs_cell,
    embed_weight,
    background,
    stencil_taps,
    weight_in,
    weight_out,
    grid_cotangent,
):
    peer_count = lax.axis_size(("tile", "stream"))
    stream = lax.axis_index("stream")
    swap = [(0, 1), (1, 0)]
    rows_dev, features = obs_rows.shape
    instr_dev = embed_weight.shape[0]
    capacity = 2 * rows_dev // peer_count
    lat_rows, lon_cells, width = grid_cotangent.shape
    band_cells = lat_rows * lon_cells
    other_weight = lax.ppermute(embed_weight, "stream", swap)
    weights = jnp.where(
        stream == 0,
        jnp.concatenate([embed_weight, other_weight], axis=0),
        jnp.concatenate([other_weight, embed_weight], axis=0),
    ).reshape(2 * instr_dev * features, width)
    destination = obs_target[:, 0]
    onehot = (destination[:, None] == jnp.arange(peer_count, dtype=jnp.int32)[None, :]).astype(
        jnp.int32
    )
    running = jnp.cumsum(onehot, axis=0)
    totals = running[-1]
    position = jnp.sum((running - onehot) * onehot, axis=1)
    slot_index = destination * capacity + position
    slot_total = peer_count * capacity
    spare = instr_dev * band_cells
    send_rows, send_codes = pack(
        slot_index, obs_instr * band_cells + obs_cell, obs_rows, slot_total
    )
    send_codes = jnp.where(
        jnp.arange(capacity, dtype=jnp.int32)[None, :] < totals[:, None],
        send_codes.reshape(peer_count, capacity),
        spare,
    )
    exchange = functools.partial(
        lax.all_to_all, axis_name=("tile", "stream"), split_axis=0, concat_axis=0, tiled=True
    )
    recv_codes = exchange(send_codes)
    recv_rows = exchange(send_rows.reshape(peer_count, capacity, features))
    held = jnp.sum((recv_codes < spare).astype(jnp.int32), axis=1)
    bounds = (jnp.max(held.reshape(-1, 2), axis=1) + 7) // 8
    recv_cells = jnp.where(recv_codes < spare, recv_codes % band_cells, band_cells)
    sums, field, density = deposit_cells(
        recv_codes.reshape(slot_total),
        recv_cells.reshape(slot_total),
        bounds,
        recv_rows.reshape(slot_total, features),
        weights,
        background,
        instr_dev,
        band_cells,
        capacity,
    )
    field = field.reshape(lat_rows, lon_cells, width)
    padded = padded_2(field, ((("tile", "stream"), 0),), 1)
    mixed = stencil(padded, stencil_taps, 1).reshape(band_cells, width)
    result, pull = jax.vjp(lambda inner: branch(inner, weight_in, weight_out), mixed)
    grid_output = (field.astype(jnp.float32) + result.reshape(lat_rows, lon_cells, width)).astype(
        jnp.bfloat16
    )
    grad_mixed = pull(grid_cotangent.reshape(band_cells, width).astype(jnp.float32))[0].astype(
        jnp.bfloat16
    )
    padded_grad = padded_2(
        grad_mixed.reshape(lat_rows, lon_cells, width), ((("tile", "stream"), 0),), 1
    )
    grad_field = grid_cotangent.astype(jnp.float32) + stencil(padded_grad, stencil_taps, -1)
    grad_cells = grad_field.reshape(band_cells, width) / density[:, :1]
    local_grad = lax.dot_general(
        sums,
        grad_cells.astype(jnp.bfloat16),
        (((0,), (0,)), ((), ())),
        preferred_element_type=jnp.float32,
    ).reshape(2, instr_dev, features, width)
    keep = jnp.where(stream == 0, local_grad[0], local_grad[1])
    give = jnp.where(stream == 0, local_grad[1], local_grad[0]).astype(jnp.bfloat16)
    group_grad = keep + lax.ppermute(give, "stream", swap).astype(jnp.float32)
    return (grid_output, sum_over_tile(group_grad))


def solution(mesh):
    in_specs = (
        P(("parts", "tile", "stream"), None),
        P(("parts", "tile", "stream")),
        P(("parts", "tile", "stream"), None),
        P(("parts", "tile", "stream")),
        P("stream", None, None),
        P(),
        P(),
        P(),
        P(),
        P(("parts", "tile", "stream"), None, None),
    )
    out_specs = (P(("parts", "tile", "stream"), None, None), P(("parts", "stream"), None, None))
    return jax.shard_map(
        on_device, mesh=mesh, in_specs=in_specs, out_specs=out_specs, check_vma=False
    )
```

profile of v0, /device:TPU:0, one launch (start us, length us, event | category | flops | bytes accessed | tf_op | source)
XLA Modules:
  0.0 320.3 jit_solution(890527210459878400)
XLA Ops:
  1.6 4.6 %reduce-window.6 = s32[16,32,128]{2,1,0:T(8,128)S(1)} reduce-window(s32[16,32,128]{2,1,0:T(8,128)S(1)} %fusion.57, s32[]{:T(128)} %constant.22.clone.1), window={size=1x1x128 pad=0_0x0_0x127_0}, to_apply=%region_0.1 | reduce-window | flops 8323072 | bytes 524292 | tf_op jit(solution)/shard_map/reduce-window
  7.0 1.9 copy.17
  9.6 2.5 select_reduce_fusion
  12.2 10.5 %shard_map.113 = (bf16[8192,128]{1,0:T(8,128)(2,1)}, s32[8192]{0:T(1024)S(1)}) custom-call(s32[4096]{0:T(1024)S(1)} %get-tuple-element.54.slot_ref, s32[4096]{0:T(1024)S(1)} %get-tuple-element.53.code_ref, bf16[4096,128]{1,0:T(8,128)(2,1)S(1)} %copy-done.2), custom_call_target="tpu_custom_call" | custom-call | tf_op jit(solution)/shard_map/pallas_call | solution.py:59
  22.9 13.8 %all_to_all.11 = s32[16,1,512]{2,1,0:T(1,128)S(1)} all-to-all(s32[16,1,512]{2,1,0:T(1,128)S(1)} %compare_select_fusion), channel_id=1, replica_groups=mesh['parts'=2,'tile'=8,'stream'=2] {'tile','stream'}, dimensions={0} | all-to-all | bytes 65536 | tf_op jit(solution)/shard_map/all_to_all | solution.py:257
  36.7 3.7 %all-to-all-start.1 = ((bf16[16,512,128]{2,1,0:T(8,128)(2,1)}), bf16[16,512,128]{2,1,0:T(8,128)(2,1)S(1)}, u32[]{:S(2)}, u32[]{:S(2)}) async-start(bf16[16,512,128]{2,1,0:T(8,128)(2,1)} %bitcast.8), calls=%async_computation.1 | async-start | bytes 4194304 | tf_op jit(solution)/shard_map/all_to_all | solution.py:258
  43.2 38.3 %all-to-all-done.1 = bf16[16,512,128]{2,1,0:T(8,128)(2,1)S(1)} async-done(((bf16[16,512,128]{2,1,0:T(8,128)(2,1)}), bf16[16,512,128]{2,1,0:T(8,128)(2,1)S(1)}, u32[]{:S(2)}, u32[]{:S(2)}) %all-to-all-start.1) | async-done | bytes 2097184 | tf_op jit(solution)/shard_map/all_to_all | solution.py:258
  82.8 22.8 %shard_map.114 = (bf16[5760,1024]{1,0:T(8,128)(2,1)}, bf16[5760,256]{1,0:T(8,128)(2,1)}, f32[5760,128]{1,0:T(8,128)}) custom-call(s32[8192]{0:T(1024)} %bitcast.73, s32[8192]{0:T(1024)} %fusion.58.cell_ref, s32[8]{0:T(128)} %and_select_fusion.bound_ref, bf16[8192,128]{1,0:T(8,128)(2,1)} %bitcast.66, bf16[1024,256]{1,0:T(8,128)(2,1)} %bitcast.71, ...), custom_call_target="tpu_custom_call" | custom-call | tf_op jit(solution)/shard_map/pallas_call | solution.py:161
  107.1 16.9 %collective-permute-start.1 = (bf16[1,1440,256]{2,1,0:T(8,128)(2,1)S(1)}, bf16[1,1440,256]{2,1,0:T(8,128)(2,1)S(1)}, u32[]{:S(2)}, u32[]{:S(2)}) collective-permute-start(bf16[1,1440,256]{2,1,0:T(8,128)(2,1)S(1)} %get-tuple-element.40), channel_id=1, source_target_pairs={{0,1},{1,2},{2,3},{3,4},{4,5},{5,6},{6,7},{7,8},{8,9},{9,10},{10,1... | collective-permute-start | bytes 2211848 | tf_op jit(solution)/shard_map/ppermute | solution.py:16
  124.0 1.5 collective-permute-start.2
  125.8 2.3 collective-permute-done.2
  129.0 2.2 maximum_convert_fusion
  131.2 12.7 %fusion.71 = (f32[4,1439,256]{2,1,0:T(8,128)}, f32[4,1439,256]{2,1,0:T(8,128)}, f32[4,1439,256]{2,1,0:T(8,128)}, f32[4,1439,256]{2,1,0:T(8,128)}, f32[4,1439,256]{2,1,0:T(8,128)}, /*index=5*/f32[4,1439,256]{2,1,0:T(8,128)}) fusion(f32[6,1440,256]{2,1,0:T(8,128)S(1)} %maximum_convert_fusion), kind=kLoop, calls=%fused_computation.135 | loop fusion | bytes 70729728 | tf_op jit(solution)/shard_map/jit(_roll_static)/slice | solution.py:196
  144.8 15.3 %multiply_reduce_fusion = (f32[4,1440]{1,0:T(4,128)S(1)}, f32[4,1440,256]{2,1,0:T(8,128)}) fusion(f32[4,1,256]{2,1,0:T(1,128)S(1)} %get-tuple-element.33, f32[4,1439,256]{2,1,0:T(8,128)} %get-tuple-element.22, f32[256]{0:T(256)S(1)} %bitcast.93, f32[6,1440,256]{2,1,0:T(8,128)S(1)} %maximum_convert_fusion, f32[256]{0:T(256)S(1)} %bitcast.95, ...), kind=kLoop, calls=%fused_computation.77 | loop fusion | flops 36858240 | bytes 59014656 | tf_op jit(solution)/shard_map/jvp()/reduce_sum | solution.py:202
  160.3 4.3 %fusion.55 = bf16[5760,256]{1,0:T(8,128)(2,1)S(1)} fusion(f32[4,1440,256]{2,1,0:T(8,128)} %get-tuple-element.13, f32[5760]{0:T(1024)S(1)} %rsqrt.10), kind=kLoop, calls=%fused_computation.74 | loop fusion | flops 2949120 | bytes 8870400 | tf_op jit(solution)/shard_map/jvp()/convert_element_type | solution.py:203
  164.5 9.5 %fusion.73 = f32[5760,1024]{1,0:T(8,128)} fusion(bf16[5760,256]{1,0:T(8,128)(2,1)S(1)} %fusion.55, bf16[256,1024]{1,0:T(8,128)(2,1)S(1)} %copy-done), kind=kOutput, calls=%fused_computation.137 | convolution fusion | flops 3019898880 | bytes 27066368 | tf_op jit(solution)/shard_map/jvp()/dot_general | solution.py:205
  174.1 22.2 %fusion.56 = (f32[5760]{0:T(1024)S(1)}, f32[5760,256]{1,0:T(8,128)}) fusion(f32[4,1440,256]{2,1,0:T(8,128)} %get-tuple-element.13, bf16[256,1024]{1,0:T(8,128)(2,1)S(1)} %copy-done, f32[5760,1024]{1,0:T(8,128)} %fusion.73, bf16[5760,256]{1,0:T(8,128)(2,1)S(1)} %bitcast.69, bf16[1024,256]{1,0:T(8,128)(2,1)} %param.18), kind=kOutput, calls=%fused_computation.75 | convolution fusion | flops 6169553408 | bytes 39410176 | tf_op jit(solution)/shard_map/transpose(jvp())/dot_general | solution.py:205
  196.3 6.6 %fusion.36 = bf16[5760,256]{1,0:T(8,128)(2,1)S(1)} fusion(f32[4,1440,256]{2,1,0:T(8,128)} %get-tuple-element.13, f32[5760,256]{1,0:T(8,128)} %get-tuple-element.52, f32[5760]{0:T(1024)S(1)} %multiply_multiply_fusion.2, f32[5760]{0:T(1024)S(1)} %rsqrt.10), kind=kLoop, calls=%fused_computation.33 | loop fusion | flops 7372800 | bytes 14791680 | tf_op jit(solution)/shard_map/convert_element_type | solution.py:280
  203.1 13.6 %collective-permute-start.3 = (bf16[1,1440,256]{2,1,0:T(8,128)(2,1)S(1)}, bf16[1,1440,256]{2,1,0:T(8,128)(2,1)S(1)}, u32[]{:S(2)}, u32[]{:S(2)}) collective-permute-start(bf16[1,1440,256]{2,1,0:T(8,128)(2,1)S(1)} %get-tuple-element.38), channel_id=1, source_target_pairs={{0,1},{1,2},{2,3},{3,4},{4,5},{5,6},{6,7},{7,8},{8,9},{9,10},{10,1... | collective-permute-start | bytes 2211848 | tf_op jit(solution)/shard_map/ppermute | solution.py:16
  218.9 3.9 %collective-permute-done.4 = bf16[1,1440,256]{2,1,0:T(8,128)(2,1)S(1)} collective-permute-done((bf16[1,1440,256]{2,1,0:T(8,128)(2,1)S(1)}, bf16[1,1440,256]{2,1,0:T(8,128)(2,1)S(1)}, u32[]{:S(2)}, u32[]{:S(2)}) %collective-permute-start.4) | collective-permute-done | bytes 737312 | tf_op jit(solution)/shard_map/ppermute | solution.py:19
  224.4 12.6 %fusion.70 = (f32[4,1439,256]{2,1,0:T(8,128)}, f32[4,1439,256]{2,1,0:T(8,128)}, f32[4,1439,256]{2,1,0:T(8,128)}, f32[4,1439,256]{2,1,0:T(8,128)}, f32[4,1439,256]{2,1,0:T(8,128)}, /*index=5*/f32[4,1439,256]{2,1,0:T(8,128)}) fusion(f32[6,1440,256]{2,1,0:T(8,128)S(1)} %maximum_convert_fusion.1), kind=kLoop, calls=%fused_computation.134 | loop fusion | bytes 70729728 | tf_op jit(solution)/shard_map/jit(_roll_static)/slice | solution.py:196
  239.0 18.0 %fusion.39 = f32[4,1440,256]{2,1,0:T(8,128)} fusion(f32[6,1440,256]{2,1,0:T(8,128)S(1)} %maximum_convert_fusion.1, f32[4,1,256]{2,1,0:T(1,128)S(1)} %get-tuple-element.31, f32[4,1439,256]{2,1,0:T(8,128)} %get-tuple-element.19, f32[4,1439,256]{2,1,0:T(8,128)} %get-tuple-element.16, f32[4,1,256]{2,1,0:T(1,128)S(1)} %get-tuple-element.30, ...), kind=kLoop, calls=%fused_computation.37 | loop fusion | flops 36864000 | bytes 61940736 | tf_op jit(solution)/shard_map/add | solution.py:286
  257.0 4.3 %fusion.54 = bf16[5760,256]{1,0:T(8,128)(2,1)S(1)} fusion(f32[4,1440,256]{2,1,0:T(8,128)} %fusion.39, f32[5760]{0:T(1024)S(1)} %slice_reduce_fusion), kind=kLoop, calls=%fused_computation.70 | loop fusion | flops 2949120 | bytes 8870400 | tf_op jit(solution)/shard_map/convert_element_type | solution.py:290
  261.3 6.3 %fusion.74 = f32[1024,256]{1,0:T(8,128)S(1)} fusion(bf16[5760,1024]{1,0:T(8,128)(2,1)} %get-tuple-element.10, bf16[5760,256]{1,0:T(8,128)(2,1)S(1)} %fusion.54), kind=kOutput, calls=%fused_computation.138 | convolution fusion | flops 3019898880 | bytes 15794176 | tf_op jit(solution)/shard_map/dot_general | solution.py:288
  267.6 13.0 %collective-permute-start.5 = (bf16[4,128,256]{2,1,0:T(8,128)(2,1)S(1)}, bf16[4,128,256]{2,1,0:T(8,128)(2,1)S(1)}, u32[]{:S(2)}, u32[]{:S(2)}) collective-permute-start(bf16[4,128,256]{2,1,0:T(8,128)(2,1)S(1)} %bitcast.74), channel_id=1, source_target_pairs={{0,1},{1,0},{2,3},{3,2},{4,5},{5,4},{6,7},{7,6},{8,9},{9,8},{10,11... | collective-permute-start | bytes 786440 | tf_op jit(solution)/shard_map/ppermute | solution.py:296
  281.8 2.8 collective-permute-start.6
  284.6 6.6 %collective-permute-done.6 = bf16[4,128,256]{2,1,0:T(8,128)(2,1)S(1)} collective-permute-done((bf16[4,128,256]{2,1,0:T(8,128)(2,1)S(1)}, bf16[4,128,256]{2,1,0:T(8,128)(2,1)S(1)}, u32[]{:S(2)}, u32[]{:S(2)}) %collective-permute-start.6) | collective-permute-done | bytes 262176 | tf_op jit(solution)/shard_map/ppermute | solution.py:182
  291.3 2.3 collective-permute-start.7
  293.7 11.6 %fusion.27 = f32[5760,256]{1,0:T(8,128)S(1)} fusion(bf16[1024,256]{1,0:T(8,128)(2,1)S(1)} %copy-done.33, f32[5760,1024]{1,0:T(8,128)} %fusion.73), kind=kOutput, calls=%fused_computation.28 | convolution fusion | flops 3072983040 | bytes 30015488 | tf_op jit(solution)/shard_map/jvp()/dot_general | solution.py:207
  305.4 2.3 collective-permute-start.8
  307.7 2.5 add_convert_fusion
  310.1 9.3 %collective-permute-done.8 = bf16[4,128,256]{2,1,0:T(8,128)(2,1)S(1)} collective-permute-done((bf16[4,128,256]{2,1,0:T(8,128)(2,1)S(1)}, bf16[4,128,256]{2,1,0:T(8,128)(2,1)S(1)}, u32[]{:S(2)}, u32[]{:S(2)}) %collective-permute-start.8) | collective-permute-done | bytes 262176 | tf_op jit(solution)/shard_map/ppermute | solution.py:182
  (106 shorter events, 18.2 us)
Async XLA Ops:
  0.6 163.9 %copy-start = (bf16[256,1024]{1,0:T(8,128)(2,1)S(1)}, bf16[256,1024]{1,0:T(8,128)(2,1)}, u32[]{:S(2)}) copy-start(bf16[256,1024]{1,0:T(8,128)(2,1)} %param.17) | copy-start | bytes 1572868
  0.7 39.7 %copy-start.14 = (bf16[4,128,256]{2,1,0:T(8,128)(2,1)S(1)}, bf16[4,128,256]{2,1,0:T(8,128)(2,1)}, u32[]{:S(2)}) copy-start(bf16[4,128,256]{2,1,0:T(8,128)(2,1)} %param.14) | copy-start | bytes 786436
  12.2 113.3 %copy-start.32 = (f32[9,256]{1,0:T(8,128)S(1)}, f32[9,256]{1,0:T(8,128)}, u32[]{:S(2)}) copy-start(f32[9,256]{1,0:T(8,128)} %param.16) | copy-start | bytes 27652
  36.7 44.8 %copy-start.13 = (s32[16,1,512]{2,1,0:T(1,128)}, s32[16,1,512]{2,1,0:T(1,128)S(1)}, u32[]{:S(2)}) copy-start(s32[16,1,512]{2,1,0:T(1,128)S(1)} %all_to_all.11) | copy-start | bytes 98308
  36.7 44.8 %all-to-all-start.1 = ((bf16[16,512,128]{2,1,0:T(8,128)(2,1)}), bf16[16,512,128]{2,1,0:T(8,128)(2,1)S(1)}, u32[]{:S(2)}, u32[]{:S(2)}) async-start(bf16[16,512,128]{2,1,0:T(8,128)(2,1)} %bitcast.8), calls=%async_computation.1 | async-start | bytes 4194304 | tf_op jit(solution)/shard_map/all_to_all | solution.py:258
  40.4 1.9 collective-permute-start
  107.1 18.7 %collective-permute-start.1 = (bf16[1,1440,256]{2,1,0:T(8,128)(2,1)S(1)}, bf16[1,1440,256]{2,1,0:T(8,128)(2,1)S(1)}, u32[]{:S(2)}, u32[]{:S(2)}) collective-permute-start(bf16[1,1440,256]{2,1,0:T(8,128)(2,1)S(1)} %get-tuple-element.40), channel_id=1, source_target_pairs={{0,1},{1,2},{2,3},{3,4},{4,5},{5,6},{6,7},{7,8},{8,9},{9,10},{10,1... | collective-permute-start | bytes 2211848 | tf_op jit(solution)/shard_map/ppermute | solution.py:16
  124.0 4.1 %collective-permute-start.2 = (bf16[1,1440,256]{2,1,0:T(8,128)(2,1)S(1)}, bf16[1,1440,256]{2,1,0:T(8,128)(2,1)S(1)}, u32[]{:S(2)}, u32[]{:S(2)}) collective-permute-start(bf16[1,1440,256]{2,1,0:T(8,128)(2,1)S(1)} %get-tuple-element.41), channel_id=1, source_target_pairs={{1,0},{2,1},{3,2},{4,3},{5,4},{6,5},{7,6},{8,7},{9,8},{10,9},{11,1... | collective-permute-start | bytes 2211848 | tf_op jit(solution)/shard_map/ppermute | solution.py:19
  125.5 19.2 %copy-start.18 = (f32[1,256]{1,0:T(1,128)}, f32[1,256]{1,0:T(1,128)S(1)}, u32[]{:S(2)}) copy-start(f32[1,256]{1,0:T(1,128)S(1)} %get-tuple-element.44) | copy-start | bytes 3076
  125.5 19.2 %copy-start.20 = (f32[1,256]{1,0:T(1,128)}, f32[1,256]{1,0:T(1,128)S(1)}, u32[]{:S(2)}) copy-start(f32[1,256]{1,0:T(1,128)S(1)} %get-tuple-element.45) | copy-start | bytes 3076
  125.5 19.2 %copy-start.22 = (f32[1,256]{1,0:T(1,128)}, f32[1,256]{1,0:T(1,128)S(1)}, u32[]{:S(2)}) copy-start(f32[1,256]{1,0:T(1,128)S(1)} %get-tuple-element.46) | copy-start | bytes 3076
  125.5 19.2 %copy-start.24 = (f32[1,256]{1,0:T(1,128)}, f32[1,256]{1,0:T(1,128)S(1)}, u32[]{:S(2)}) copy-start(f32[1,256]{1,0:T(1,128)S(1)} %get-tuple-element.47) | copy-start | bytes 3076
  125.5 19.2 %copy-start.26 = (f32[1,256]{1,0:T(1,128)}, f32[1,256]{1,0:T(1,128)S(1)}, u32[]{:S(2)}) copy-start(f32[1,256]{1,0:T(1,128)S(1)} %get-tuple-element.48) | copy-start | bytes 3076
  125.5 19.2 %copy-start.28 = (f32[1,256]{1,0:T(1,128)}, f32[1,256]{1,0:T(1,128)S(1)}, u32[]{:S(2)}) copy-start(f32[1,256]{1,0:T(1,128)S(1)} %get-tuple-element.49) | copy-start | bytes 3076
  125.6 19.2 %copy-start.30 = (f32[1,256]{1,0:T(1,128)}, f32[1,256]{1,0:T(1,128)S(1)}, u32[]{:S(2)}) copy-start(f32[1,256]{1,0:T(1,128)S(1)} %get-tuple-element.50) | copy-start | bytes 3076
  196.3 21.7 %copy-start.6 = (f32[5760,128]{1,0:T(8,128)S(1)}, f32[5760,128]{1,0:T(8,128)}, u32[]{:S(2)}) copy-start(f32[5760,128]{1,0:T(8,128)} %get-tuple-element.11) | copy-start | bytes 8847364
  203.0 19.8 %copy-start.4 = (bf16[5760,256]{1,0:T(8,128)(2,1)}, bf16[5760,256]{1,0:T(8,128)(2,1)S(1)}, u32[]{:S(2)}) copy-start(bf16[5760,256]{1,0:T(8,128)(2,1)S(1)} %fusion.36) | copy-start | bytes 8847364
  203.1 15.8 %collective-permute-start.3 = (bf16[1,1440,256]{2,1,0:T(8,128)(2,1)S(1)}, bf16[1,1440,256]{2,1,0:T(8,128)(2,1)S(1)}, u32[]{:S(2)}, u32[]{:S(2)}) collective-permute-start(bf16[1,1440,256]{2,1,0:T(8,128)(2,1)S(1)} %get-tuple-element.38), channel_id=1, source_target_pairs={{0,1},{1,2},{2,3},{3,4},{4,5},{5,6},{6,7},{7,8},{8,9},{9,10},{10,1... | collective-permute-start | bytes 2211848 | tf_op jit(solution)/shard_map/ppermute | solution.py:16
  216.8 6.0 %collective-permute-start.4 = (bf16[1,1440,256]{2,1,0:T(8,128)(2,1)S(1)}, bf16[1,1440,256]{2,1,0:T(8,128)(2,1)S(1)}, u32[]{:S(2)}, u32[]{:S(2)}) collective-permute-start(bf16[1,1440,256]{2,1,0:T(8,128)(2,1)S(1)} %get-tuple-element.39), channel_id=1, source_target_pairs={{1,0},{2,1},{3,2},{4,3},{5,4},{6,5},{7,6},{8,7},{9,8},{10,9},{11,1... | collective-permute-start | bytes 2211848 | tf_op jit(solution)/shard_map/ppermute | solution.py:19
  224.4 13.7 %copy-start.19 = (f32[1,256]{1,0:T(1,128)S(1)}, f32[1,256]{1,0:T(1,128)}, u32[]{:S(2)}) copy-start(f32[1,256]{1,0:T(1,128)} %copy-done.18) | copy-start | bytes 3076
  224.4 13.7 %copy-start.21 = (f32[1,256]{1,0:T(1,128)S(1)}, f32[1,256]{1,0:T(1,128)}, u32[]{:S(2)}) copy-start(f32[1,256]{1,0:T(1,128)} %copy-done.20) | copy-start | bytes 3076
  224.4 13.7 %copy-start.23 = (f32[1,256]{1,0:T(1,128)S(1)}, f32[1,256]{1,0:T(1,128)}, u32[]{:S(2)}) copy-start(f32[1,256]{1,0:T(1,128)} %copy-done.22) | copy-start | bytes 3076
  224.4 13.7 %copy-start.25 = (f32[1,256]{1,0:T(1,128)S(1)}, f32[1,256]{1,0:T(1,128)}, u32[]{:S(2)}) copy-start(f32[1,256]{1,0:T(1,128)} %copy-done.24) | copy-start | bytes 3076
  224.4 13.7 %copy-start.27 = (f32[1,256]{1,0:T(1,128)S(1)}, f32[1,256]{1,0:T(1,128)}, u32[]{:S(2)}) copy-start(f32[1,256]{1,0:T(1,128)} %copy-done.26) | copy-start | bytes 3076
  224.4 13.7 %copy-start.29 = (f32[1,256]{1,0:T(1,128)S(1)}, f32[1,256]{1,0:T(1,128)}, u32[]{:S(2)}) copy-start(f32[1,256]{1,0:T(1,128)} %copy-done.28) | copy-start | bytes 3076
  224.4 13.7 %copy-start.31 = (f32[1,256]{1,0:T(1,128)S(1)}, f32[1,256]{1,0:T(1,128)}, u32[]{:S(2)}) copy-start(f32[1,256]{1,0:T(1,128)} %copy-done.30) | copy-start | bytes 3076
  261.3 32.4 %copy-start.33 = (bf16[1024,256]{1,0:T(8,128)(2,1)S(1)}, bf16[1024,256]{1,0:T(8,128)(2,1)}, u32[]{:S(2)}) copy-start(bf16[1024,256]{1,0:T(8,128)(2,1)} %param.18) | copy-start | bytes 1572868
  267.6 14.1 %collective-permute-start.5 = (bf16[4,128,256]{2,1,0:T(8,128)(2,1)S(1)}, bf16[4,128,256]{2,1,0:T(8,128)(2,1)S(1)}, u32[]{:S(2)}, u32[]{:S(2)}) collective-permute-start(bf16[4,128,256]{2,1,0:T(8,128)(2,1)S(1)} %bitcast.74), channel_id=1, source_target_pairs={{0,1},{1,0},{2,3},{3,2},{4,5},{5,4},{6,7},{7,6},{8,9},{9,8},{10,11... | collective-permute-start | bytes 786440 | tf_op jit(solution)/shard_map/ppermute | solution.py:296
  281.8 9.4 %collective-permute-start.6 = (bf16[4,128,256]{2,1,0:T(8,128)(2,1)S(1)}, bf16[4,128,256]{2,1,0:T(8,128)(2,1)S(1)}, u32[]{:S(2)}, u32[]{:S(2)}) collective-permute-start(bf16[4,128,256]{2,1,0:T(8,128)(2,1)S(1)} %add_convert_fusion.3), channel_id=1, source_target_pairs={{0,2},{2,0},{4,6},{6,4},{8,10},{10,8},{12,14},{14,12},{1,3},{3,1},... | collective-permute-start | bytes 786440 | tf_op jit(solution)/shard_map/ppermute | solution.py:182
  291.3 16.3 %copy-start.3 = (bf16[5760,256]{1,0:T(8,128)(2,1)S(1)}, bf16[5760,256]{1,0:T(8,128)(2,1)}, u32[]{:S(2)}) copy-start(bf16[5760,256]{1,0:T(8,128)(2,1)} %get-tuple-element.9) | copy-start | bytes 8847364
  291.3 14.0 %collective-permute-start.7 = (bf16[4,128,256]{2,1,0:T(8,128)(2,1)S(1)}, bf16[4,128,256]{2,1,0:T(8,128)(2,1)S(1)}, u32[]{:S(2)}, u32[]{:S(2)}) collective-permute-start(bf16[4,128,256]{2,1,0:T(8,128)(2,1)S(1)} %add_convert_fusion.2), channel_id=1, source_target_pairs={{0,4},{2,6},{4,0},{6,2},{8,12},{10,14},{12,8},{14,10},{1,5},{3,7},... | collective-permute-start | bytes 786440 | tf_op jit(solution)/shard_map/ppermute | solution.py:182
  305.4 14.0 %collective-permute-start.8 = (bf16[4,128,256]{2,1,0:T(8,128)(2,1)S(1)}, bf16[4,128,256]{2,1,0:T(8,128)(2,1)S(1)}, u32[]{:S(2)}, u32[]{:S(2)}) collective-permute-start(bf16[4,128,256]{2,1,0:T(8,128)(2,1)S(1)} %add_convert_fusion.1), channel_id=1, source_target_pairs={{0,8},{2,10},{4,12},{6,14},{8,0},{10,2},{12,4},{14,6},{1,9},{3,11}... | collective-permute-start | bytes 786440 | tf_op jit(solution)/shard_map/ppermute | solution.py:182
  (12 other events, 79.5 us)
where the time goes:
time: 324 us; the launch traced here: 320 us
  other arithmetic  67.6 us (21%)
  waiting for transfers between devices  61.6 us (19%)
  starting transfers between devices  57.8 us (18%)
  matrix products  49.7 us (15%)
  local copies, waits for them, and re-layouts  35.1 us (11%)
  Pallas kernels  33.3 us (10%)
  blocking collectives  13.8 us (4%)
    all_to_all x1, waiting for transfers between devices, on_device(): recv_rows = exchange(send_rows.reshape(peer_count, capacity, features))  38.3 us
    dot_general x2, matrix products, branch(): jnp.dot(normed, weight_in, preferred_element_type=jnp.float32)  31.8 us
    ppermute x2, starting transfers between devices, padded_2(): lax.ppermute(lax.slice_in_dim(block, block.shape[dim] - width, None, axis...  30.6 us
    slice x2, local copies, waits for them, and re-layouts, stencil(): window = jnp.roll(window, -orient * (col_step - 1), axis=1)  25.3 us
    pallas_call x1, Pallas kernels, deposit_cells(): pl.pallas_call(functools.partial(deposit_kernel, instr_dev, capacity), ou...  22.8 us
    add x1, other arithmetic, on_device(): grid_cotangent.astype(jnp.float32) + stencil(padded_grad, stencil_taps, -1)  18 us
    ppermute x3, waiting for transfers between devices, sum_over_tile(): lax.ppermute(mine, 'tile', [(i, i ^ distance) for i in range(count)])  15.9 us
    reduce_sum x1, other arithmetic, branch(): jnp.mean(mixed * mixed, axis=-1, keepdims=True) + 1e-06  15.3 us
  transfers between devices with their start and end apart: 10, of which 7 were waited for; matrix products, arithmetic and copies ran while one was open for 5% of the time, Pallas kernels for 0%

commit v1 on v0

--- a/solution.py
+++ b/solution.py
@@ -8,17 +8,12 @@
 from jax.sharding import PartitionSpec as P
 
 
-def padded_2(block, sides, width):
-    for axis, dim in sides:
-        count = lax.axis_size(axis)
-        forward = [(i, i + 1) for i in range(count - 1)]
-        backward = [(target, source) for source, target in forward]
-        low = lax.ppermute(
-            lax.slice_in_dim(block, block.shape[dim] - width, None, axis=dim), axis, forward
-        )
-        high = lax.ppermute(lax.slice_in_dim(block, 0, width, axis=dim), axis, backward)
-        block = jnp.concatenate([low, block, high], axis=dim)
-    return block
+def edge_rows(block):
+    axes = ("tile", "stream")
+    count = lax.axis_size(axes)
+    forward = [(i, i + 1) for i in range(count - 1)]
+    backward = [(target, source) for source, target in forward]
+    return lax.ppermute(block[-1:], axes, forward), lax.ppermute(block[:1], axes, backward)
 
 
 def pack_kernel(slot_ref, code_ref, rows_ref, out_rows, out_codes, rows_wide, packed):
@@ -185,26 +180,137 @@
     return value
 
 
-def stencil(padded, stencil_taps, orient):
-    row_count = padded.shape[0] - 2
-    field = padded.astype(jnp.float32)
-    summed = jnp.zeros((row_count,) + padded.shape[1:], jnp.float32)
-    for row_step in range(3):
-        for col_step in range(3):
-            offset = 1 + orient * (row_step - 1)
-            window = lax.slice_in_dim(field, offset, offset + row_count, axis=0)
-            window = jnp.roll(window, -orient * (col_step - 1), axis=1)
-            summed = summed + stencil_taps[row_step * 3 + col_step] * window
-    return summed
-
-
-def branch(mixed, weight_in, weight_out):
-    inverse_rms = lax.rsqrt(jnp.mean(mixed * mixed, axis=-1, keepdims=True) + 1e-06)
-    normed = (mixed * inverse_rms).astype(jnp.bfloat16)
-    hidden = jax.nn.gelu(
-        jnp.dot(normed, weight_in, preferred_element_type=jnp.float32), approximate=True
-    ).astype(jnp.bfloat16)
-    return jnp.dot(hidden, weight_out, preferred_element_type=jnp.float32)
+HALO = 16
+CHUNK = 288
+
+
+def fill_padded(padded, low_ref, block_ref, high_ref):
+    rows, columns = block_ref.shape[0], block_ref.shape[1]
+    for row in range(rows + 2):
+        if row == 0:
+            source, at = low_ref, 0
+        elif row == rows + 1:
+            source, at = high_ref, 0
+        else:
+            source, at = block_ref, row - 1
+        padded[row, HALO : HALO + columns, :] = source[at]
+        padded[row, 0:HALO, :] = source[at, columns - HALO : columns, :]
+        padded[row, HALO + columns : 2 * HALO + columns, :] = source[at, 0:HALO, :]
+
+
+def stencil(padded, taps_ref, row, start, orient):
+    size = CHUNK + 2 * HALO
+    rows = [
+        padded[row + step, pl.ds(start, size), :].astype(jnp.float32) for step in range(3)
+    ]
+    total = None
+    for col_step in range(3):
+        summed = None
+        for row_step in range(3):
+            tap = taps_ref[pl.ds(row_step * 3 + col_step, 1), :]
+            term = tap * rows[1 + orient * (row_step - 1)]
+            summed = term if summed is None else summed + term
+        shift = -orient * (col_step - 1)
+        if shift:
+            summed = pltpu.roll(summed, shift % size, 0)
+        summed = summed[HALO : HALO + CHUNK]
+        total = summed if total is None else total + summed
+    return total
+
+
+def layer_kernel(
+    low_ref,
+    field_ref,
+    high_ref,
+    taps_ref,
+    in_ref,
+    out_ref,
+    in_t_ref,
+    out_t_ref,
+    cot_ref,
+    grid_ref,
+    grad_ref,
+    padded,
+):
+    fill_padded(padded, low_ref, field_ref, high_ref)
+    rows, columns = field_ref.shape[0], field_ref.shape[1]
+    pieces = columns // CHUNK
+
+    @pl.loop(0, rows * pieces)
+    def _(index):
+        row = index // pieces
+        start = pl.multiple_of((index % pieces) * CHUNK, 32)
+        at = pl.ds(start, CHUNK)
+        mixed = stencil(padded, taps_ref, row, start, 1)
+        inverse = lax.rsqrt(jnp.mean(mixed * mixed, axis=1, keepdims=True) + 1e-06)
+        normed = (mixed * inverse).astype(jnp.bfloat16)
+        inner = jnp.dot(normed, in_ref[...], preferred_element_type=jnp.float32)
+        cot = cot_ref[row, at, :]
+        grad_hidden = jnp.dot(cot, out_t_ref[...], preferred_element_type=jnp.float32)
+        grad_hidden = grad_hidden.astype(jnp.bfloat16).astype(jnp.float32)
+        scale = 0.7978845608028654
+        square = inner * inner
+        bent = jnp.tanh(inner * (scale + (scale * 0.044715) * square))
+        half = 0.5 + 0.5 * bent
+        hidden = (inner * half).astype(jnp.bfloat16)
+        slope = (2.0 * scale) + (6.0 * scale * 0.044715) * square
+        grad_inner = grad_hidden * (half + inner * (half - half * half) * slope)
+        result = jnp.dot(hidden, out_ref[...], preferred_element_type=jnp.float32)
+        grid_ref[row, at, :] = (field_ref[row, at, :].astype(jnp.float32) + result).astype(
+            jnp.bfloat16
+        )
+        grad_normed = jnp.dot(
+            grad_inner.astype(jnp.bfloat16), in_t_ref[...], preferred_element_type=jnp.float32
+        )
+        grad_normed = grad_normed.astype(jnp.bfloat16).astype(jnp.float32)
+        along = jnp.mean(mixed * grad_normed, axis=1, keepdims=True)
+        grad_mixed = inverse * grad_normed - mixed * (along * (inverse * inverse * inverse))
+        grad_ref[row, at, :] = grad_mixed.astype(jnp.bfloat16)
+
+
+def layer(edges, field, taps, weight_in, weight_out, cotangent):
+    rows, columns, width = field.shape
+    vmem = pl.BlockSpec(memory_space=pltpu.VMEM)
+    shape = jax.ShapeDtypeStruct(field.shape, jnp.bfloat16)
+    return pl.pallas_call(
+        layer_kernel,
+        out_shape=(shape, shape),
+        in_specs=[vmem] * 9,
+        out_specs=(vmem, vmem),
+        scratch_shapes=[pltpu.VMEM((rows + 2, columns + 2 * HALO, width), jnp.bfloat16)],
+        compiler_params=pltpu.CompilerParams(vmem_limit_bytes=40 << 20),
+    )(edges[0], field, edges[1], taps, weight_in, weight_out, weight_in.T, weight_out.T, cotangent)
+
+
+def back_kernel(low_ref, grad_ref, high_ref, taps_ref, cot_ref, density_ref, cells_ref, padded):
+    fill_padded(padded, low_ref, grad_ref, high_ref)
+    rows, columns = grad_ref.shape[0], grad_ref.shape[1]
+    pieces = columns // CHUNK
+
+    @pl.loop(0, rows * pieces)
+    def _(index):
+        row = index // pieces
+        start = pl.multiple_of((index % pieces) * CHUNK, 32)
+        at = pl.ds(start, CHUNK)
+        cells = pl.ds(pl.multiple_of(index * CHUNK, 32), CHUNK)
+        grad = stencil(padded, taps_ref, row, start, -1)
+        grad = cot_ref[row, at, :].astype(jnp.float32) + grad
+        density = density_ref[cells, :]
+        density = jnp.concatenate([density] * (grad.shape[1] // density.shape[1]), axis=1)
+        cells_ref[cells, :] = (grad / density).astype(jnp.bfloat16)
+
+
+def back(edges, grad_mixed, taps, cotangent, density):
+    rows, columns, width = grad_mixed.shape
+    vmem = pl.BlockSpec(memory_space=pltpu.VMEM)
+    return pl.pallas_call(
+        back_kernel,
+        out_shape=jax.ShapeDtypeStruct((rows * columns, width), jnp.bfloat16),
+        in_specs=[vmem] * 6,
+        out_specs=vmem,
+        scratch_shapes=[pltpu.VMEM((rows + 2, columns + 2 * HALO, width), jnp.bfloat16)],
+        compiler_params=pltpu.CompilerParams(vmem_limit_bytes=40 << 20),
+    )(edges[0], grad_mixed, edges[1], taps, cotangent, density)
 
 
 def on_device(
@@ -271,23 +377,13 @@
         capacity,
     )
     field = field.reshape(lat_rows, lon_cells, width)
-    padded = padded_2(field, ((("tile", "stream"), 0),), 1)
-    mixed = stencil(padded, stencil_taps, 1).reshape(band_cells, width)
-    result, pull = jax.vjp(lambda inner: branch(inner, weight_in, weight_out), mixed)
-    grid_output = (field.astype(jnp.float32) + result.reshape(lat_rows, lon_cells, width)).astype(
-        jnp.bfloat16
-    )
-    grad_mixed = pull(grid_cotangent.reshape(band_cells, width).astype(jnp.float32))[0].astype(
-        jnp.bfloat16
-    )
-    padded_grad = padded_2(
-        grad_mixed.reshape(lat_rows, lon_cells, width), ((("tile", "stream"), 0),), 1
-    )
-    grad_field = grid_cotangent.astype(jnp.float32) + stencil(padded_grad, stencil_taps, -1)
-    grad_cells = grad_field.reshape(band_cells, width) / density[:, :1]
+    grid_output, grad_mixed = layer(
+        edge_rows(field), field, stencil_taps, weight_in, weight_out, grid_cotangent
+    )
+    grad_cells = back(edge_rows(grad_mixed), grad_mixed, stencil_taps, grid_cotangent, density)
     local_grad = lax.dot_general(
         sums,
-        grad_cells.astype(jnp.bfloat16),
+        grad_cells,
         (((0,), (0,)), ((), ())),
         preferred_element_type=jnp.float32,
     ).reshape(2, instr_dev, features, width)

time: 324 us -> 250 us (0.77)
  other arithmetic: 67.6 us -> 10.8 us
  matrix products: 49.7 us -> 6.22 us
  Pallas kernels: 33.3 us -> 75.6 us
  local copies, waits for them, and re-layouts: 35.1 us -> 13.3 us
  starting transfers between devices: 57.8 us -> 62.1 us
  waiting for transfers between devices: 61.6 us -> 65 us
    dot_general x4 -> x1, matrix products: 49.7 us -> 6.22 us  [on_device(): lax.dot_general(sums, grad_cells, (((0,), (0,)), ((), ())), preferred_ele...]
    pallas_call x0 -> x2, Pallas kernels: none -> 40.7 us  [the longest x1 34.6 us: layer(): pl.pallas_call(layer_kernel, out_shape=(shape, shape), in_specs=[vmem] *...]
    slice x6 -> x3, local copies, waits for them, and re-layouts: 27.7 us -> 3.25 us  [the longest x2 2.79 us: edge_rows(): block[:1]]
    convert_element_type x6 -> x0, other arithmetic: 20.5 us -> none  [the longest x1 6.63 us: on_device(): pull(grid_cotangent.reshape(band_cells, width).astype(jnp.float32))[0]]
    ppermute x3, starting transfers between devices: 7.4 us -> 26.4 us  [sum_over_tile(): lax.ppermute(mine, 'tile', [(i, i ^ distance) for i in range(count)])]
    add x2 -> x0, other arithmetic: 18 us -> none  [the longest x1 18 us: on_device(): grid_cotangent.astype(jnp.float32) + stencil(padded_grad, stencil_taps, -1)]
    reduce_sum x1 -> x0, other arithmetic: 15.3 us -> none  [branch(): jnp.mean(mixed * mixed, axis=-1, keepdims=True) + 1e-06]
    ppermute x4, starting transfers between devices: 33.3 us -> 21.1 us  [the longest x2 18.2 us: edge_rows(): lax.ppermute(block[-1:], axes, forward)]
  transfers between devices with their start and end apart: 10 -> 10, of which waited for: 7 -> 6; matrix products, arithmetic and copies ran while one was open for 5% -> 2% of each run, Pallas kernels for 0% -> 0%
where the time goes in v1:
time: 250 us; the launch traced here: 248 us
  Pallas kernels  75.6 us (30%)
  waiting for transfers between devices  65 us (26%)
  starting transfers between devices  62.1 us (25%)
  blocking collectives  13.8 us (6%)
  local copies, waits for them, and re-layouts  13.3 us (5%)
  other arithmetic  10.8 us (4%)
  matrix products  6.22 us (2%)
    all_to_all x1, waiting for transfers between devices, on_device(): recv_rows = exchange(send_rows.reshape(peer_count, capacity, features))  38.3 us
    pallas_call x1, Pallas kernels, layer(): pl.pallas_call(layer_kernel, out_shape=(shape, shape), in_specs=[vmem] *...  34.6 us
    ppermute x3, starting transfers between devices, sum_over_tile(): lax.ppermute(mine, 'tile', [(i, i ^ distance) for i in range(count)])  26.4 us
    pallas_call x1, Pallas kernels, deposit_cells(): pl.pallas_call(functools.partial(deposit_kernel, instr_dev, capacity), ou...  24.3 us
    ppermute x3, waiting for transfers between devices, sum_over_tile(): lax.ppermute(mine, 'tile', [(i, i ^ distance) for i in range(count)])  23.9 us
    ppermute x2, starting transfers between devices, edge_rows(): lax.ppermute(block[-1:], axes, forward)  18.2 us
    all_to_all x1, blocking collectives, on_device(): recv_codes = exchange(send_codes)  13.8 us
    ppermute x1, starting transfers between devices, on_device(): group_grad = keep + lax.ppermute(give, 'stream', swap).astype(jnp.float32)  10.6 us
  transfers between devices with their start and end apart: 10, of which 6 were waited for; matrix products, arithmetic and copies ran while one was open for 2% of the time, Pallas kernels for 0%

profile of v1, /device:TPU:0, one launch (start us, length us, event | category | flops | bytes accessed | tf_op | source)
XLA Modules:
  0.0 247.7 jit_solution(8023188526006894948)
XLA Ops:
  1.5 4.6 %reduce-window.6 = s32[16,32,128]{2,1,0:T(8,128)S(1)} reduce-window(s32[16,32,128]{2,1,0:T(8,128)S(1)} %fusion, s32[]{:T(128)} %constant.35.clone.1), window={size=1x1x128 pad=0_0x0_0x127_0}, to_apply=%region_0.1 | reduce-window | flops 8323072 | bytes 524292 | tf_op jit(solution)/shard_map/reduce-window
  7.5 1.4 select_reduce_fusion
  9.0 10.5 %shard_map.113 = (bf16[8192,128]{1,0:T(8,128)(2,1)}, s32[8192]{0:T(1024)S(1)}) custom-call(s32[4096]{0:T(1024)S(1)} %get-tuple-element.21.slot_ref, s32[4096]{0:T(1024)S(1)} %get-tuple-element.20.code_ref, bf16[4096,128]{1,0:T(8,128)(2,1)S(1)} %copy-done.7), custom_call_target="tpu_custom_call" | custom-call | tf_op jit(solution)/shard_map/pallas_call | solution.py:54
  19.7 13.8 %all_to_all.11 = s32[16,1,512]{2,1,0:T(1,128)S(1)} all-to-all(s32[16,1,512]{2,1,0:T(1,128)S(1)} %compare_select_fusion), channel_id=1, replica_groups=mesh['parts'=2,'tile'=8,'stream'=2] {'tile','stream'}, dimensions={0} | all-to-all | bytes 65536 | tf_op jit(solution)/shard_map/all_to_all | solution.py:363
  33.5 3.7 %all-to-all-start.1 = ((bf16[16,512,128]{2,1,0:T(8,128)(2,1)}), bf16[16,512,128]{2,1,0:T(8,128)(2,1)S(1)}, u32[]{:S(2)}, u32[]{:S(2)}) async-start(bf16[16,512,128]{2,1,0:T(8,128)(2,1)} %bitcast.8), calls=%async_computation.1 | async-start | bytes 4194304 | tf_op jit(solution)/shard_map/all_to_all | solution.py:364
  39.1 0.9 maximum_select_fusion
  40.0 38.3 %all-to-all-done.1 = bf16[16,512,128]{2,1,0:T(8,128)(2,1)S(1)} async-done(((bf16[16,512,128]{2,1,0:T(8,128)(2,1)}), bf16[16,512,128]{2,1,0:T(8,128)(2,1)S(1)}, u32[]{:S(2)}, u32[]{:S(2)}) %all-to-all-start.1) | async-done | bytes 2097184 | tf_op jit(solution)/shard_map/all_to_all | solution.py:364
  78.3 1.3 copy-done.9
  79.6 24.3 %shard_map.114 = (bf16[5760,1024]{1,0:T(8,128)(2,1)}, bf16[5760,256]{1,0:T(8,128)(2,1)}, f32[5760,128]{1,0:T(8,128)}) custom-call(s32[8192]{0:T(1024)} %bitcast.35, s32[8192]{0:T(1024)} %fusion.1.cell_ref, s32[8]{0:T(128)} %and_select_fusion.bound_ref, bf16[8192,128]{1,0:T(8,128)(2,1)} %bitcast.30, bf16[1024,256]{1,0:T(8,128)(2,1)} %bitcast.33, ...), custom_call_target="tpu_custom_call" | custom-call | tf_op jit(solution)/shard_map/pallas_call | solution.py:156
  103.9 2.7 %slice_bitcast_fusion = (bf16[1,1440,256]{2,1,0:T(8,128)(2,1)}, bf16[1,1440,256]{2,1,0:T(8,128)(2,1)}) fusion(bf16[5760,256]{1,0:T(8,128)(2,1)} %get-tuple-element.11), kind=kLoop, calls=%fused_computation.2 | loop fusion | bytes 2949120 | tf_op jit(solution)/shard_map/slice | solution.py:16
  106.6 1.3 collective-permute-start.2
  107.9 3.9 %collective-permute-start.1 = (bf16[1,1440,256]{2,1,0:T(8,128)(2,1)}, bf16[1,1440,256]{2,1,0:T(8,128)(2,1)}, u32[]{:S(2)}, u32[]{:S(2)}) collective-permute-start(bf16[1,1440,256]{2,1,0:T(8,128)(2,1)} %get-tuple-element.19), channel_id=1, source_target_pairs={{0,1},{1,2},{2,3},{3,4},{4,5},{5,6},{6,7},{7,8},{8,9},{9,10},{10,1... | collective-permute-start | bytes 2211848 | tf_op jit(solution)/shard_map/ppermute | solution.py:16
  111.8 1.0 copy.23
  112.8 2.0 copy.24
  114.9 1.8 copy-done.1
  116.7 1.0 copy-done.4
  117.8 1.0 copy-done.5
  118.8 1.0 copy-done.6
  119.9 34.6 %shard_map.115 = (bf16[4,1440,256]{2,1,0:T(8,128)(2,1)}, bf16[4,1440,256]{2,1,0:T(8,128)(2,1)S(1)}) custom-call(bf16[1,1440,256]{2,1,0:T(8,128)(2,1)} %collective-permute-done.1.low_ref, bf16[4,1440,256]{2,1,0:T(8,128)(2,1)S(1)} %bitcast.26, bf16[1,1440,256]{2,1,0:T(8,128)(2,1)} %collective-permute-done.2.high_ref, f32[9,256]{1,0:T(8,128)S(1)} %copy-done.8, ...), custom_call_target="tpu_custom_call" | custom-call | tf_op jit(solution)/shard_map/pallas_call | solution.py:275
  154.6 1.6 collective-permute-start.4
  156.2 14.3 %collective-permute-start.3 = (bf16[1,1440,256]{2,1,0:T(8,128)(2,1)S(1)}, bf16[1,1440,256]{2,1,0:T(8,128)(2,1)S(1)}, u32[]{:S(2)}, u32[]{:S(2)}) collective-permute-start(bf16[1,1440,256]{2,1,0:T(8,128)(2,1)S(1)} %get-tuple-element.17), channel_id=1, source_target_pairs={{0,1},{1,2},{2,3},{3,4},{4,5},{5,6},{6,7},{7,8},{8,9},{9,10},{10,1... | collective-permute-start | bytes 2211848 | tf_op jit(solution)/shard_map/ppermute | solution.py:16
  170.5 1.8 collective-permute-done.3.low_ref
  172.3 6.1 %shard_map.116 = bf16[5760,256]{1,0:T(8,128)(2,1)S(1)} custom-call(bf16[1,1440,256]{2,1,0:T(8,128)(2,1)S(1)} %collective-permute-done.3.low_ref, bf16[4,1440,256]{2,1,0:T(8,128)(2,1)S(1)} %get-tuple-element.14.grad_ref, bf16[1,1440,256]{2,1,0:T(8,128)(2,1)S(1)} %collective-permute-done.4.high_ref, f32[9,256]{1,0:T(8,128)S(1)} %copy-done.8, ...), custom_call_target="tpu_custom_call" | custom-call | tf_op jit(solution)/shard_map/pallas_call | solution.py:306
  178.4 6.2 %fusion.3 = f32[1024,256]{1,0:T(8,128)S(1)} fusion(bf16[5760,1024]{1,0:T(8,128)(2,1)} %get-tuple-element.13, bf16[5760,256]{1,0:T(8,128)(2,1)S(1)} %shard_map.116), kind=kOutput, calls=%fused_computation.28 | convolution fusion | flops 3019898880 | bytes 15794176 | tf_op jit(solution)/shard_map/dot_general | solution.py:384
  184.6 10.6 %collective-permute-start.5 = (bf16[4,128,256]{2,1,0:T(8,128)(2,1)S(1)}, bf16[4,128,256]{2,1,0:T(8,128)(2,1)S(1)}, u32[]{:S(2)}, u32[]{:S(2)}) collective-permute-start(bf16[4,128,256]{2,1,0:T(8,128)(2,1)S(1)} %bitcast.36), channel_id=1, source_target_pairs={{0,1},{1,0},{2,3},{3,2},{4,5},{5,4},{6,7},{7,6},{8,9},{9,8},{10,11... | collective-permute-start | bytes 786440 | tf_op jit(solution)/shard_map/ppermute | solution.py:392
  195.3 1.1 collective-permute-done.5
  196.5 11.7 %collective-permute-start.6 = (bf16[4,128,256]{2,1,0:T(8,128)(2,1)S(1)}, bf16[4,128,256]{2,1,0:T(8,128)(2,1)S(1)}, u32[]{:S(2)}, u32[]{:S(2)}) collective-permute-start(bf16[4,128,256]{2,1,0:T(8,128)(2,1)S(1)} %add_convert_fusion.2), channel_id=1, source_target_pairs={{0,2},{2,0},{4,6},{6,4},{8,10},{10,8},{12,14},{14,12},{1,3},{3,1},... | collective-permute-start | bytes 786440 | tf_op jit(solution)/shard_map/ppermute | solution.py:177
  208.2 6.8 %collective-permute-done.6 = bf16[4,128,256]{2,1,0:T(8,128)(2,1)S(1)} collective-permute-done((bf16[4,128,256]{2,1,0:T(8,128)(2,1)S(1)}, bf16[4,128,256]{2,1,0:T(8,128)(2,1)S(1)}, u32[]{:S(2)}, u32[]{:S(2)}) %collective-permute-start.6) | collective-permute-done | bytes 262176 | tf_op jit(solution)/shard_map/ppermute | solution.py:177
  215.1 8.8 %collective-permute-start.7 = (bf16[4,128,256]{2,1,0:T(8,128)(2,1)S(1)}, bf16[4,128,256]{2,1,0:T(8,128)(2,1)S(1)}, u32[]{:S(2)}, u32[]{:S(2)}) collective-permute-start(bf16[4,128,256]{2,1,0:T(8,128)(2,1)S(1)} %add_convert_fusion.1), channel_id=1, source_target_pairs={{0,4},{2,6},{4,0},{6,2},{8,12},{10,14},{12,8},{14,10},{1,5},{3,7},... | collective-permute-start | bytes 786440 | tf_op jit(solution)/shard_map/ppermute | solution.py:177
  224.0 6.0 %collective-permute-done.7 = bf16[4,128,256]{2,1,0:T(8,128)(2,1)S(1)} collective-permute-done((bf16[4,128,256]{2,1,0:T(8,128)(2,1)S(1)}, bf16[4,128,256]{2,1,0:T(8,128)(2,1)S(1)}, u32[]{:S(2)}, u32[]{:S(2)}) %collective-permute-start.7) | collective-permute-done | bytes 262176 | tf_op jit(solution)/shard_map/ppermute | solution.py:177
  230.1 5.8 %collective-permute-start.8 = (bf16[4,128,256]{2,1,0:T(8,128)(2,1)S(1)}, bf16[4,128,256]{2,1,0:T(8,128)(2,1)S(1)}, u32[]{:S(2)}, u32[]{:S(2)}) collective-permute-start(bf16[4,128,256]{2,1,0:T(8,128)(2,1)S(1)} %add_convert_fusion), channel_id=1, source_target_pairs={{0,8},{2,10},{4,12},{6,14},{8,0},{10,2},{12,4},{14,6},{1,9},{3,11}... | collective-permute-start | bytes 786440 | tf_op jit(solution)/shard_map/ppermute | solution.py:177
  235.8 11.1 %collective-permute-done.8 = bf16[4,128,256]{2,1,0:T(8,128)(2,1)S(1)} collective-permute-done((bf16[4,128,256]{2,1,0:T(8,128)(2,1)S(1)}, bf16[4,128,256]{2,1,0:T(8,128)(2,1)S(1)}, u32[]{:S(2)}, u32[]{:S(2)}) %collective-permute-start.8) | collective-permute-done | bytes 262176 | tf_op jit(solution)/shard_map/ppermute | solution.py:177
  (51 shorter events, 5.5 us)
Async XLA Ops:
  0.6 6.9 %copy-start.12 = (s32[4096,1]{0,1:T(1,128)S(1)}, s32[4096,1]{0,1:T(1,128)}, u32[]{:S(2)}) copy-start(s32[4096,1]{0,1:T(1,128)} %param.12) | copy-start | bytes 49156
  1.4 7.5 %copy-start.13 = (s32[4096]{0:T(1024)S(1)}, s32[4096]{0:T(1024)}, u32[]{:S(2)}) copy-start(s32[4096]{0:T(1024)} %param.13) | copy-start | bytes 49156
  1.5 7.5 %copy-start.14 = (s32[4096]{0:T(1024)S(1)}, s32[4096]{0:T(1024)}, u32[]{:S(2)}) copy-start(s32[4096]{0:T(1024)} %param.11) | copy-start | bytes 49156
  1.5 7.6 %copy-start.7 = (bf16[4096,128]{1,0:T(8,128)(2,1)S(1)}, bf16[4096,128]{1,0:T(8,128)(2,1)}, u32[]{:S(2)}) copy-start(bf16[4096,128]{1,0:T(8,128)(2,1)} %rows_ref.1) | copy-start | bytes 3145732
  9.0 28.2 %copy-start.11 = (bf16[4,128,256]{2,1,0:T(8,128)(2,1)S(1)}, bf16[4,128,256]{2,1,0:T(8,128)(2,1)}, u32[]{:S(2)}) copy-start(bf16[4,128,256]{2,1,0:T(8,128)(2,1)} %param.14) | copy-start | bytes 786436
  33.5 44.8 %copy-start.10 = (s32[16,1,512]{2,1,0:T(1,128)}, s32[16,1,512]{2,1,0:T(1,128)S(1)}, u32[]{:S(2)}) copy-start(s32[16,1,512]{2,1,0:T(1,128)S(1)} %all_to_all.11) | copy-start | bytes 98308
  33.5 44.8 %all-to-all-start.1 = ((bf16[16,512,128]{2,1,0:T(8,128)(2,1)}), bf16[16,512,128]{2,1,0:T(8,128)(2,1)S(1)}, u32[]{:S(2)}, u32[]{:S(2)}) async-start(bf16[16,512,128]{2,1,0:T(8,128)(2,1)} %bitcast.8), calls=%async_computation.1 | async-start | bytes 4194304 | tf_op jit(solution)/shard_map/all_to_all | solution.py:364
  37.3 1.9 collective-permute-start
  40.0 71.8 %copy-start.3 = (bf16[256,1024]{1,0:T(8,128)(2,1)S(1)}, bf16[256,1024]{1,0:T(8,128)(2,1)}, u32[]{:S(2)}) copy-start(bf16[256,1024]{1,0:T(8,128)(2,1)} %in_ref.1) | copy-start | bytes 1572868
  78.3 1.3 copy-start.9
  103.9 11.0 %copy-start = (bf16[4,1440,256]{2,1,0:T(8,128)(2,1)S(1)}, bf16[4,1440,256]{2,1,0:T(8,128)(2,1)}, u32[]{:S(2)}) copy-start(bf16[4,1440,256]{2,1,0:T(8,128)(2,1)} %cot_ref.3) | copy-start | bytes 8847364
  103.9 11.0 %copy-start.8 = (f32[9,256]{1,0:T(8,128)S(1)}, f32[9,256]{1,0:T(8,128)}, u32[]{:S(2)}) copy-start(f32[9,256]{1,0:T(8,128)} %taps_ref.3) | copy-start | bytes 27652
  106.6 8.3 %collective-permute-start.2 = (bf16[1,1440,256]{2,1,0:T(8,128)(2,1)}, bf16[1,1440,256]{2,1,0:T(8,128)(2,1)}, u32[]{:S(2)}, u32[]{:S(2)}) collective-permute-start(bf16[1,1440,256]{2,1,0:T(8,128)(2,1)} %get-tuple-element.18), channel_id=1, source_target_pairs={{1,0},{2,1},{3,2},{4,3},{5,4},{6,5},{7,6},{8,7},{9,8},{10,9},{11,1... | collective-permute-start | bytes 2211848 | tf_op jit(solution)/shard_map/ppermute | solution.py:16
  107.9 7.0 %collective-permute-start.1 = (bf16[1,1440,256]{2,1,0:T(8,128)(2,1)}, bf16[1,1440,256]{2,1,0:T(8,128)(2,1)}, u32[]{:S(2)}, u32[]{:S(2)}) collective-permute-start(bf16[1,1440,256]{2,1,0:T(8,128)(2,1)} %get-tuple-element.19), channel_id=1, source_target_pairs={{0,1},{1,2},{2,3},{3,4},{4,5},{5,6},{6,7},{7,8},{8,9},{9,10},{10,1... | collective-permute-start | bytes 2211848 | tf_op jit(solution)/shard_map/ppermute | solution.py:16
  114.9 1.8 copy-start.1
  116.7 1.0 copy-start.4
  117.8 1.0 copy-start.5
  118.8 1.0 copy-start.6
  154.5 17.8 %copy-start.2 = (f32[5760,128]{1,0:T(8,128)S(1)}, f32[5760,128]{1,0:T(8,128)}, u32[]{:S(2)}) copy-start(f32[5760,128]{1,0:T(8,128)} %get-tuple-element.15.density_ref) | copy-start | bytes 8847364
  154.6 15.9 %collective-permute-start.4 = (bf16[1,1440,256]{2,1,0:T(8,128)(2,1)S(1)}, bf16[1,1440,256]{2,1,0:T(8,128)(2,1)S(1)}, u32[]{:S(2)}, u32[]{:S(2)}) collective-permute-start(bf16[1,1440,256]{2,1,0:T(8,128)(2,1)S(1)} %get-tuple-element.16), channel_id=1, source_target_pairs={{1,0},{2,1},{3,2},{4,3},{5,4},{6,5},{7,6},{8,7},{9,8},{10,9},{11,1... | collective-permute-start | bytes 2211848 | tf_op jit(solution)/shard_map/ppermute | solution.py:16
  156.2 16.1 %collective-permute-start.3 = (bf16[1,1440,256]{2,1,0:T(8,128)(2,1)S(1)}, bf16[1,1440,256]{2,1,0:T(8,128)(2,1)S(1)}, u32[]{:S(2)}, u32[]{:S(2)}) collective-permute-start(bf16[1,1440,256]{2,1,0:T(8,128)(2,1)S(1)} %get-tuple-element.17), channel_id=1, source_target_pairs={{0,1},{1,2},{2,3},{3,4},{4,5},{5,6},{6,7},{7,8},{8,9},{9,10},{10,1... | collective-permute-start | bytes 2211848 | tf_op jit(solution)/shard_map/ppermute | solution.py:16
  184.6 11.8 %collective-permute-start.5 = (bf16[4,128,256]{2,1,0:T(8,128)(2,1)S(1)}, bf16[4,128,256]{2,1,0:T(8,128)(2,1)S(1)}, u32[]{:S(2)}, u32[]{:S(2)}) collective-permute-start(bf16[4,128,256]{2,1,0:T(8,128)(2,1)S(1)} %bitcast.36), channel_id=1, source_target_pairs={{0,1},{1,0},{2,3},{3,2},{4,5},{5,4},{6,7},{7,6},{8,9},{9,8},{10,11... | collective-permute-start | bytes 786440 | tf_op jit(solution)/shard_map/ppermute | solution.py:392
  196.5 18.6 %collective-permute-start.6 = (bf16[4,128,256]{2,1,0:T(8,128)(2,1)S(1)}, bf16[4,128,256]{2,1,0:T(8,128)(2,1)S(1)}, u32[]{:S(2)}, u32[]{:S(2)}) collective-permute-start(bf16[4,128,256]{2,1,0:T(8,128)(2,1)S(1)} %add_convert_fusion.2), channel_id=1, source_target_pairs={{0,2},{2,0},{4,6},{6,4},{8,10},{10,8},{12,14},{14,12},{1,3},{3,1},... | collective-permute-start | bytes 786440 | tf_op jit(solution)/shard_map/ppermute | solution.py:177
  215.1 14.9 %collective-permute-start.7 = (bf16[4,128,256]{2,1,0:T(8,128)(2,1)S(1)}, bf16[4,128,256]{2,1,0:T(8,128)(2,1)S(1)}, u32[]{:S(2)}, u32[]{:S(2)}) collective-permute-start(bf16[4,128,256]{2,1,0:T(8,128)(2,1)S(1)} %add_convert_fusion.1), channel_id=1, source_target_pairs={{0,4},{2,6},{4,0},{6,2},{8,12},{10,14},{12,8},{14,10},{1,5},{3,7},... | collective-permute-start | bytes 786440 | tf_op jit(solution)/shard_map/ppermute | solution.py:177
  230.1 16.8 %collective-permute-start.8 = (bf16[4,128,256]{2,1,0:T(8,128)(2,1)S(1)}, bf16[4,128,256]{2,1,0:T(8,128)(2,1)S(1)}, u32[]{:S(2)}, u32[]{:S(2)}) collective-permute-start(bf16[4,128,256]{2,1,0:T(8,128)(2,1)S(1)} %add_convert_fusion), channel_id=1, source_target_pairs={{0,8},{2,10},{4,12},{6,14},{8,0},{10,2},{12,4},{14,6},{1,9},{3,11}... | collective-permute-start | bytes 786440 | tf_op jit(solution)/shard_map/ppermute | solution.py:177

commit v2 on v1

--- a/solution.py
+++ b/solution.py
@@ -70,6 +70,7 @@
 def deposit_kernel(
     instr_dev,
     capacity,
+    pitch,
     code_ref,
     cell_ref,
     bound_ref,
@@ -88,7 +89,7 @@
 ):
     cells = field_out.shape[0]
     features = rows_ref.shape[1]
-    pairs = rows_ref.shape[0] // (2 * capacity)
+    pairs = rows_ref.shape[0] // (2 * pitch)
     step = 480
 
     @pl.loop(0, instr_dev * cells // step)
@@ -110,8 +111,10 @@
     def _(pair):
         first = pl.multiple_of(pair * 2 * capacity, capacity)
         second = pl.multiple_of(first + capacity, capacity)
-        even_rows[...] = rows_ref[pl.ds(first, capacity), :].astype(jnp.float32)
-        odd_rows[...] = rows_ref[pl.ds(second, capacity), :].astype(jnp.float32)
+        even_at = pl.multiple_of(pair * 2 * pitch, 16)
+        odd_at = pl.multiple_of(even_at + pitch, 16)
+        even_rows[...] = rows_ref[pl.ds(even_at, capacity), :].astype(jnp.float32)
+        odd_rows[...] = rows_ref[pl.ds(odd_at, capacity), :].astype(jnp.float32)
 
         @pl.loop(0, bound_ref[pair])
         def _(block):
@@ -145,7 +148,9 @@
         field_out[at, :] = ((deposit + background_ref[...]) / density).astype(jnp.bfloat16)
 
 
-def deposit_cells(codes, cells, bounds, rows, weights, background, instr_dev, band_cells, capacity):
+def deposit_cells(
+    codes, cells, bounds, rows, weights, background, instr_dev, band_cells, capacity, pitch
+):
     features = rows.shape[1]
     width = weights.shape[1]
     smem = pl.BlockSpec(memory_space=pltpu.SMEM)
@@ -154,7 +159,7 @@
     counts = pltpu.VMEM((band_cells + 8, features), jnp.float32)
     held = pltpu.VMEM((capacity, features), jnp.float32)
     return pl.pallas_call(
-        functools.partial(deposit_kernel, instr_dev, capacity),
+        functools.partial(deposit_kernel, instr_dev, capacity, pitch),
         out_shape=(
             jax.ShapeDtypeStruct((band_cells, weights.shape[0]), jnp.bfloat16),
             jax.ShapeDtypeStruct((band_cells, width), jnp.bfloat16),
@@ -167,17 +172,21 @@
     )(codes, cells, bounds, rows, weights, background.reshape(1, width))
 
 
-def sum_over_tile(value):
+def gathered_over_tile(piece):
     count = lax.axis_size("tile")
     if count & (count - 1):
-        return lax.psum(value.astype(jnp.bfloat16), "tile").astype(jnp.float32)
-    distance = 1
-    while distance < count:
-        mine = value.astype(jnp.bfloat16)
-        other = lax.ppermute(mine, "tile", [(i, i ^ distance) for i in range(count)])
-        value = mine.astype(jnp.float32) + other.astype(jnp.float32)
-        distance *= 2
-    return value
+        return lax.all_gather(piece, "tile")
+    me = lax.axis_index("tile")
+    distance, axis, block = count // 2, 0, piece
+    while distance:
+        other = lax.ppermute(block, "tile", [(i, i ^ distance) for i in range(count)])
+        upper = (me & distance) > 0
+        block = jnp.stack(
+            [jnp.where(upper, other, block), jnp.where(upper, block, other)], axis=axis
+        )
+        axis += 1
+        distance //= 2
+    return block.reshape((count,) + piece.shape)
 
 
 HALO = 16
@@ -357,11 +366,28 @@
         send_codes.reshape(peer_count, capacity),
         spare,
     )
-    exchange = functools.partial(
-        lax.all_to_all, axis_name=("tile", "stream"), split_axis=0, concat_axis=0, tiled=True
-    )
-    recv_codes = exchange(send_codes)
-    recv_rows = exchange(send_rows.reshape(peer_count, capacity, features))
+    code_rows = capacity // features
+    padding = -2 * code_rows % 16
+    coded = jnp.concatenate(
+        [
+            (send_codes // 256).reshape(peer_count, code_rows, features),
+            (send_codes % 256).reshape(peer_count, code_rows, features),
+            jnp.zeros((peer_count, padding, features), jnp.int32),
+        ],
+        axis=1,
+    ).astype(jnp.bfloat16)
+    recv_rows = lax.all_to_all(
+        jnp.concatenate([send_rows.reshape(peer_count, capacity, features), coded], axis=1),
+        ("tile", "stream"),
+        split_axis=0,
+        concat_axis=0,
+        tiled=True,
+    )
+    pitch = capacity + 2 * code_rows + padding
+    digits = recv_rows[:, capacity : capacity + 2 * code_rows].astype(jnp.int32)
+    recv_codes = (digits[:, :code_rows] * 256 + digits[:, code_rows:]).reshape(
+        peer_count, capacity
+    )
     held = jnp.sum((recv_codes < spare).astype(jnp.int32), axis=1)
     bounds = (jnp.max(held.reshape(-1, 2), axis=1) + 7) // 8
     recv_cells = jnp.where(recv_codes < spare, recv_codes % band_cells, band_cells)
@@ -369,12 +395,13 @@
         recv_codes.reshape(slot_total),
         recv_cells.reshape(slot_total),
         bounds,
-        recv_rows.reshape(slot_total, features),
+        recv_rows.reshape(peer_count * pitch, features),
         weights,
         background,
         instr_dev,
         band_cells,
         capacity,
+        pitch,
     )
     field = field.reshape(lat_rows, lon_cells, width)
     grid_output, grad_mixed = layer(
@@ -386,11 +413,19 @@
         grad_cells,
         (((0,), (0,)), ((), ())),
         preferred_element_type=jnp.float32,
-    ).reshape(2, instr_dev, features, width)
-    keep = jnp.where(stream == 0, local_grad[0], local_grad[1])
-    give = jnp.where(stream == 0, local_grad[1], local_grad[0]).astype(jnp.bfloat16)
-    group_grad = keep + lax.ppermute(give, "stream", swap).astype(jnp.float32)
-    return (grid_output, sum_over_tile(group_grad))
+    )
+    tiles = peer_count // 2
+    shares = local_grad.astype(jnp.bfloat16).reshape(2, tiles, -1, width)
+    shares = lax.all_to_all(
+        jnp.swapaxes(shares, 0, 1).reshape(peer_count, -1, width),
+        ("tile", "stream"),
+        split_axis=0,
+        concat_axis=0,
+        tiled=True,
+    )
+    piece = jnp.sum(shares.astype(jnp.float32), axis=0).astype(jnp.bfloat16)
+    embed_grad = gathered_over_tile(piece).astype(jnp.float32)
+    return (grid_output, embed_grad.reshape(embed_weight.shape))
 
 
 def solution(mesh):

time: 250 us -> 245 us (0.980)
  starting transfers between devices: 62.1 us -> 25.1 us
  blocking collectives: 13.8 us -> 40 us
  Pallas kernels: 75.6 us -> 88.4 us
  waiting for transfers between devices: 65 us -> 55.7 us
    ppermute x4 -> x3, starting transfers between devices: 37 us -> 2.99 us  [gathered_over_tile(): lax.ppermute(block, 'tile', [(i, i ^ distance) for i in range(count)])]
    all_to_all x1, blocking collectives: 13.8 us -> 40 us  [on_device(): lax.all_to_all(jnp.swapaxes(shares, 0, 1).reshape(peer_count, -1, width),...]
    ppermute x4 -> x3, waiting for transfers between devices: 25 us -> 11.9 us  [gathered_over_tile(): lax.ppermute(block, 'tile', [(i, i ^ distance) for i in range(count)])]
    pallas_call x1, Pallas kernels: 24.3 us -> 37.3 us  [deposit_cells(): pl.pallas_call(functools.partial(deposit_kernel, instr_dev, capacity, pit...]
    ppermute x2, starting transfers between devices: 18.2 us -> 11.5 us  [edge_rows(): lax.ppermute(block[-1:], axes, forward)]
    all_to_all x1, starting transfers between devices: 3.72 us -> 7.52 us  [on_device(): lax.all_to_all(jnp.concatenate([send_rows.reshape(peer_count, capacity, f...]
    another operation x3 -> x10, other arithmetic: 4.95 us -> 5.19 us
  transfers between devices with their start and end apart: 10 -> 9, of which waited for: 6 -> 8; matrix products, arithmetic and copies ran while one was open for 2% -> 2% of each run, Pallas kernels for 0% -> 0%
where the time goes in v2:
time: 245 us; the launch traced here: 241 us
  Pallas kernels  88.4 us (36%)
  waiting for transfers between devices  55.7 us (23%)
  blocking collectives  40 us (16%)
  starting transfers between devices  25.1 us (10%)
  other arithmetic  12.8 us (5%)
  local copies, waits for them, and re-layouts  12.1 us (5%)
  matrix products  6.4 us (3%)
    all_to_all x1, blocking collectives, on_device(): lax.all_to_all(jnp.swapaxes(shares, 0, 1).reshape(peer_count, -1, width),...  40 us
    all_to_all x1, waiting for transfers between devices, on_device(): lax.all_to_all(jnp.concatenate([send_rows.reshape(peer_count, capacity, f...  39.7 us
    pallas_call x1, Pallas kernels, deposit_cells(): pl.pallas_call(functools.partial(deposit_kernel, instr_dev, capacity, pit...  37.3 us
    pallas_call x1, Pallas kernels, layer(): pl.pallas_call(layer_kernel, out_shape=(shape, shape), in_specs=[vmem] *...  34.6 us
    ppermute x3, waiting for transfers between devices, gathered_over_tile(): lax.ppermute(block, 'tile', [(i, i ^ distance) for i in range(count)])  11.9 us
    ppermute x2, starting transfers between devices, edge_rows(): lax.ppermute(block[-1:], axes, forward)  11.5 us
    pallas_call x1, Pallas kernels, pack(): pl.pallas_call(pack_kernel, out_shape=(jax.ShapeDtypeStruct((slot_total,...  10.3 us
    unnamed x32, local copies, waits for them, and re-layouts  8.07 us
  transfers between devices with their start and end apart: 9, of which 8 were waited for; matrix products, arithmetic and copies ran while one was open for 2% of the time, Pallas kernels for 0%

profile of v2, /device:TPU:0, one launch (start us, length us, event | category | flops | bytes accessed | tf_op | source)
XLA Modules:
  0.0 241.4 jit_solution(8871126063490384324)
XLA Ops:
  0.7 0.8 fusion
  1.5 4.6 %reduce-window.6 = s32[16,32,128]{2,1,0:T(8,128)S(1)} reduce-window(s32[16,32,128]{2,1,0:T(8,128)S(1)} %fusion, s32[]{:T(128)} %constant.68.clone.1), window={size=1x1x128 pad=0_0x0_0x127_0}, to_apply=%region_0.1 | reduce-window | flops 8323072 | bytes 524292 | tf_op jit(solution)/shard_map/reduce-window
  7.5 1.4 select_reduce_fusion
  9.1 10.3 %shard_map.113 = (bf16[8192,128]{1,0:T(8,128)(2,1)S(1)}, s32[8192]{0:T(1024)S(1)}) custom-call(s32[4096]{0:T(1024)S(1)} %get-tuple-element.31.slot_ref, s32[4096]{0:T(1024)S(1)} %get-tuple-element.30.code_ref, bf16[4096,128]{1,0:T(8,128)(2,1)S(1)} %copy-done.7), custom_call_target="tpu_custom_call" | custom-call | tf_op jit(solution)/shard_map/pallas_call | solution.py:54
  19.6 1.9 maximum_maximum_fusion
  21.4 7.5 %all-to-all-start = ((bf16[16,528,128]{2,1,0:T(8,128)(2,1)}), bf16[16,528,128]{2,1,0:T(8,128)(2,1)S(1)}, u32[]{:S(2)}, u32[]{:S(2)}) async-start(bf16[16,528,128]{2,1,0:T(8,128)(2,1)} %maximum_maximum_fusion), calls=%async_computation | async-start | bytes 4325376 | tf_op jit(solution)/shard_map/all_to_all | solution.py:379
  29.4 1.2 collective-permute-done
  30.6 0.9 maximum_select_fusion
  31.5 39.7 %all-to-all-done = bf16[16,528,128]{2,1,0:T(8,128)(2,1)S(1)} async-done(((bf16[16,528,128]{2,1,0:T(8,128)(2,1)}), bf16[16,528,128]{2,1,0:T(8,128)(2,1)S(1)}, u32[]{:S(2)}, u32[]{:S(2)}) %all-to-all-start) | async-done | bytes 2162720 | tf_op jit(solution)/shard_map/all_to_all | solution.py:379
  71.6 0.6 fusion.3.cell_ref
  73.1 37.3 %shard_map.114 = (bf16[5760,1024]{1,0:T(8,128)(2,1)}, bf16[5760,256]{1,0:T(8,128)(2,1)}, f32[5760,128]{1,0:T(8,128)}) custom-call(s32[8192]{0:T(1024)} %bitcast.58, s32[8192]{0:T(1024)} %fusion.3.cell_ref, s32[8]{0:T(128)} %and_select_fusion.bound_ref, bf16[8448,128]{1,0:T(8,128)(2,1)} %bitcast.51, bf16[1024,256]{1,0:T(8,128)(2,1)} %bitcast.54, ...), custom_call_target="tpu_custom_call" | custom-call | tf_op jit(solution)/shard_map/pallas_call | solution.py:161
  110.4 2.7 %slice_bitcast_fusion = (bf16[1,1440,256]{2,1,0:T(8,128)(2,1)}, bf16[1,1440,256]{2,1,0:T(8,128)(2,1)}) fusion(bf16[5760,256]{1,0:T(8,128)(2,1)} %get-tuple-element.11), kind=kLoop, calls=%fused_computation.4 | loop fusion | bytes 2949120 | tf_op jit(solution)/shard_map/slice | solution.py:16
  113.1 2.2 collective-permute-start.1
  115.3 1.3 collective-permute-start.2
  116.6 1.0 copy.18
  117.6 2.1 copy.19
  119.7 1.8 copy-done.1
  121.6 1.0 copy-done.4
  122.6 1.0 copy-done.5
  123.6 1.0 copy-done.6
  124.7 34.6 %shard_map.115 = (bf16[4,1440,256]{2,1,0:T(8,128)(2,1)}, bf16[4,1440,256]{2,1,0:T(8,128)(2,1)S(1)}) custom-call(bf16[1,1440,256]{2,1,0:T(8,128)(2,1)} %collective-permute-done.1.low_ref, bf16[4,1440,256]{2,1,0:T(8,128)(2,1)S(1)} %bitcast.46, bf16[1,1440,256]{2,1,0:T(8,128)(2,1)} %collective-permute-done.2.high_ref, f32[9,256]{1,0:T(8,128)S(1)} %copy-done.8, ...), custom_call_target="tpu_custom_call" | custom-call | tf_op jit(solution)/shard_map/pallas_call | solution.py:284
  159.4 9.4 %collective-permute-start.3 = (bf16[1,1440,256]{2,1,0:T(8,128)(2,1)S(1)}, bf16[1,1440,256]{2,1,0:T(8,128)(2,1)S(1)}, u32[]{:S(2)}, u32[]{:S(2)}) collective-permute-start(bf16[1,1440,256]{2,1,0:T(8,128)(2,1)S(1)} %get-tuple-element.19), channel_id=1, source_target_pairs={{0,1},{1,2},{2,3},{3,4},{4,5},{5,6},{6,7},{7,8},{8,9},{9,10},{10,1... | collective-permute-start | bytes 2211848 | tf_op jit(solution)/shard_map/ppermute | solution.py:16
  168.8 1.3 collective-permute-start.4
  170.6 2.3 collective-permute-done.4.high_ref
  172.9 6.1 %shard_map.116 = bf16[5760,256]{1,0:T(8,128)(2,1)S(1)} custom-call(bf16[1,1440,256]{2,1,0:T(8,128)(2,1)S(1)} %collective-permute-done.3.low_ref, bf16[4,1440,256]{2,1,0:T(8,128)(2,1)S(1)} %get-tuple-element.14.grad_ref, bf16[1,1440,256]{2,1,0:T(8,128)(2,1)S(1)} %collective-permute-done.4.high_ref, f32[9,256]{1,0:T(8,128)S(1)} %copy-done.8, ...), custom_call_target="tpu_custom_call" | custom-call | tf_op jit(solution)/shard_map/pallas_call | solution.py:315
  179.0 6.4 %convolution_convert_fusion = bf16[1024,256]{1,0:T(8,128)(2,1)S(1)} fusion(bf16[5760,1024]{1,0:T(8,128)(2,1)} %get-tuple-element.13, bf16[5760,256]{1,0:T(8,128)(2,1)S(1)} %shard_map.116), kind=kOutput, calls=%fused_computation.3 | convolution fusion | flops 3020161024 | bytes 15269888 | tf_op jit(solution)/shard_map/dot_general | solution.py:411
  185.4 40.0 %all_to_all.10 = bf16[16,64,256]{2,1,0:T(8,128)(2,1)S(1)} all-to-all(bf16[16,64,256]{2,1,0:T(8,128)(2,1)S(1)} %bitcast.53), channel_id=1, replica_groups=mesh['parts'=2,'tile'=8,'stream'=2] {'tile','stream'}, dimensions={0} | all-to-all | bytes 1048576 | tf_op jit(solution)/shard_map/all_to_all | solution.py:419
  225.5 2.3 collective-permute-start.5
  227.8 3.3 %collective-permute-done.5 = bf16[64,256]{1,0:T(8,128)(2,1)S(1)} collective-permute-done((bf16[64,256]{1,0:T(8,128)(2,1)S(1)}, bf16[64,256]{1,0:T(8,128)(2,1)S(1)}, u32[]{:S(2)}, u32[]{:S(2)}) %collective-permute-start.5) | collective-permute-done | bytes 32800 | tf_op jit(solution)/shard_map/ppermute | solution.py:182
  231.7 3.7 %collective-permute-done.6 = bf16[2,64,256]{2,1,0:T(8,128)(2,1)S(1)} collective-permute-done((bf16[2,64,256]{2,1,0:T(8,128)(2,1)S(1)}, bf16[2,64,256]{2,1,0:T(8,128)(2,1)S(1)}, u32[]{:S(2)}, u32[]{:S(2)}) %collective-permute-start.6) | collective-permute-done | bytes 65568 | tf_op jit(solution)/shard_map/ppermute | solution.py:182
  235.6 4.9 %collective-permute-done.7 = bf16[2,2,64,256]{3,2,1,0:T(8,128)(2,1)S(1)} collective-permute-done((bf16[2,2,64,256]{3,2,1,0:T(8,128)(2,1)S(1)}, bf16[2,2,64,256]{3,2,1,0:T(8,128)(2,1)S(1)}, u32[]{:S(2)}, u32[]{:S(2)}) %collective-permute-start.7) | collective-permute-done | bytes 131104 | tf_op jit(solution)/shard_map/ppermute | solution.py:182
  240.6 0.8 convert.12
  (56 shorter events, 4.9 us)
Async XLA Ops:
  0.6 6.9 %copy-start.12 = (s32[4096,1]{0,1:T(1,128)S(1)}, s32[4096,1]{0,1:T(1,128)}, u32[]{:S(2)}) copy-start(s32[4096,1]{0,1:T(1,128)} %param.12) | copy-start | bytes 49156
  1.4 7.6 %copy-start.13 = (s32[4096]{0:T(1024)S(1)}, s32[4096]{0:T(1024)}, u32[]{:S(2)}) copy-start(s32[4096]{0:T(1024)} %param.13) | copy-start | bytes 49156
  1.5 7.6 %copy-start.14 = (s32[4096]{0:T(1024)S(1)}, s32[4096]{0:T(1024)}, u32[]{:S(2)}) copy-start(s32[4096]{0:T(1024)} %param.11) | copy-start | bytes 49156
  1.5 7.6 %copy-start.7 = (bf16[4096,128]{1,0:T(8,128)(2,1)S(1)}, bf16[4096,128]{1,0:T(8,128)(2,1)}, u32[]{:S(2)}) copy-start(bf16[4096,128]{1,0:T(8,128)(2,1)} %rows_ref.1) | copy-start | bytes 3145732
  21.4 7.5 %copy-start.11 = (bf16[4,128,256]{2,1,0:T(8,128)(2,1)S(1)}, bf16[4,128,256]{2,1,0:T(8,128)(2,1)}, u32[]{:S(2)}) copy-start(bf16[4,128,256]{2,1,0:T(8,128)(2,1)} %param.14) | copy-start | bytes 786436
  21.4 49.8 %all-to-all-start = ((bf16[16,528,128]{2,1,0:T(8,128)(2,1)}), bf16[16,528,128]{2,1,0:T(8,128)(2,1)S(1)}, u32[]{:S(2)}, u32[]{:S(2)}) async-start(bf16[16,528,128]{2,1,0:T(8,128)(2,1)} %maximum_maximum_fusion), calls=%async_computation | async-start | bytes 4325376 | tf_op jit(solution)/shard_map/all_to_all | solution.py:379
  29.0 1.6 collective-permute-start
  71.2 1.9 copy-start.9
  71.2 45.3 %copy-start.3 = (bf16[256,1024]{1,0:T(8,128)(2,1)S(1)}, bf16[256,1024]{1,0:T(8,128)(2,1)}, u32[]{:S(2)}) copy-start(bf16[256,1024]{1,0:T(8,128)(2,1)} %in_ref.1) | copy-start | bytes 1572868
  71.6 1.5 copy-start.10
  110.4 9.3 %copy-start = (bf16[4,1440,256]{2,1,0:T(8,128)(2,1)S(1)}, bf16[4,1440,256]{2,1,0:T(8,128)(2,1)}, u32[]{:S(2)}) copy-start(bf16[4,1440,256]{2,1,0:T(8,128)(2,1)} %cot_ref.3) | copy-start | bytes 8847364
  110.4 9.3 %copy-start.8 = (f32[9,256]{1,0:T(8,128)S(1)}, f32[9,256]{1,0:T(8,128)}, u32[]{:S(2)}) copy-start(f32[9,256]{1,0:T(8,128)} %taps_ref.3) | copy-start | bytes 27652
  113.1 6.5 %collective-permute-start.1 = (bf16[1,1440,256]{2,1,0:T(8,128)(2,1)}, bf16[1,1440,256]{2,1,0:T(8,128)(2,1)}, u32[]{:S(2)}, u32[]{:S(2)}) collective-permute-start(bf16[1,1440,256]{2,1,0:T(8,128)(2,1)} %get-tuple-element.21), channel_id=1, source_target_pairs={{0,1},{1,2},{2,3},{3,4},{4,5},{5,6},{6,7},{7,8},{8,9},{9,10},{10,1... | collective-permute-start | bytes 2211848 | tf_op jit(solution)/shard_map/ppermute | solution.py:16
  115.3 4.4 %collective-permute-start.2 = (bf16[1,1440,256]{2,1,0:T(8,128)(2,1)}, bf16[1,1440,256]{2,1,0:T(8,128)(2,1)}, u32[]{:S(2)}, u32[]{:S(2)}) collective-permute-start(bf16[1,1440,256]{2,1,0:T(8,128)(2,1)} %get-tuple-element.20), channel_id=1, source_target_pairs={{1,0},{2,1},{3,2},{4,3},{5,4},{6,5},{7,6},{8,7},{9,8},{10,9},{11,1... | collective-permute-start | bytes 2211848 | tf_op jit(solution)/shard_map/ppermute | solution.py:16
  119.7 1.8 copy-start.1
  121.6 1.0 copy-start.4
  122.6 1.0 copy-start.5
  123.6 1.0 copy-start.6
  159.3 13.6 %copy-start.2 = (f32[5760,128]{1,0:T(8,128)S(1)}, f32[5760,128]{1,0:T(8,128)}, u32[]{:S(2)}) copy-start(f32[5760,128]{1,0:T(8,128)} %get-tuple-element.15.density_ref) | copy-start | bytes 8847364
  159.4 11.1 %collective-permute-start.3 = (bf16[1,1440,256]{2,1,0:T(8,128)(2,1)S(1)}, bf16[1,1440,256]{2,1,0:T(8,128)(2,1)S(1)}, u32[]{:S(2)}, u32[]{:S(2)}) collective-permute-start(bf16[1,1440,256]{2,1,0:T(8,128)(2,1)S(1)} %get-tuple-element.19), channel_id=1, source_target_pairs={{0,1},{1,2},{2,3},{3,4},{4,5},{5,6},{6,7},{7,8},{8,9},{9,10},{10,1... | collective-permute-start | bytes 2211848 | tf_op jit(solution)/shard_map/ppermute | solution.py:16
  168.8 4.1 %collective-permute-start.4 = (bf16[1,1440,256]{2,1,0:T(8,128)(2,1)S(1)}, bf16[1,1440,256]{2,1,0:T(8,128)(2,1)S(1)}, u32[]{:S(2)}, u32[]{:S(2)}) collective-permute-start(bf16[1,1440,256]{2,1,0:T(8,128)(2,1)S(1)} %get-tuple-element.18), channel_id=1, source_target_pairs={{1,0},{2,1},{3,2},{4,3},{5,4},{6,5},{7,6},{8,7},{9,8},{10,9},{11,1... | collective-permute-start | bytes 2211848 | tf_op jit(solution)/shard_map/ppermute | solution.py:16
  225.5 5.6 %collective-permute-start.5 = (bf16[64,256]{1,0:T(8,128)(2,1)S(1)}, bf16[64,256]{1,0:T(8,128)(2,1)S(1)}, u32[]{:S(2)}, u32[]{:S(2)}) collective-permute-start(bf16[64,256]{1,0:T(8,128)(2,1)S(1)} %reduce_sum.32), channel_id=1, source_target_pairs={{0,8},{2,10},{4,12},{6,14},{8,0},{10,2},{12,4},{14,6},{1,9},{3,11}... | collective-permute-start | bytes 98312 | tf_op jit(solution)/shard_map/ppermute | solution.py:182
  231.1 4.3 %collective-permute-start.6 = (bf16[2,64,256]{2,1,0:T(8,128)(2,1)S(1)}, bf16[2,64,256]{2,1,0:T(8,128)(2,1)S(1)}, u32[]{:S(2)}, u32[]{:S(2)}) collective-permute-start(bf16[2,64,256]{2,1,0:T(8,128)(2,1)S(1)} %pad_maximum_fusion.2), channel_id=1, source_target_pairs={{0,4},{2,6},{4,0},{6,2},{8,12},{10,14},{12,8},{14,10},{1,5},{3,7},... | collective-permute-start | bytes 196616 | tf_op jit(solution)/shard_map/ppermute | solution.py:182
  235.5 5.0 %collective-permute-start.7 = (bf16[2,2,64,256]{3,2,1,0:T(8,128)(2,1)S(1)}, bf16[2,2,64,256]{3,2,1,0:T(8,128)(2,1)S(1)}, u32[]{:S(2)}, u32[]{:S(2)}) collective-permute-start(bf16[2,2,64,256]{3,2,1,0:T(8,128)(2,1)S(1)} %pad_maximum_fusion.1), channel_id=1, source_target_pairs={{0,2},{2,0},{4,6},{6,4},{8,10},{10,8},{12,14},{14,12},{1,3},{3,1},... | collective-permute-start | bytes 393224 | tf_op jit(solution)/shard_map/ppermute | solution.py:182

commit v3 on v2

--- a/solution.py
+++ b/solution.py
@@ -8,12 +8,12 @@
 from jax.sharding import PartitionSpec as P
 
 
-def edge_rows(block):
+def edge_rows(first, last):
     axes = ("tile", "stream")
     count = lax.axis_size(axes)
     forward = [(i, i + 1) for i in range(count - 1)]
     backward = [(target, source) for source, target in forward]
-    return lax.ppermute(block[-1:], axes, forward), lax.ppermute(block[:1], axes, backward)
+    return lax.ppermute(last, axes, forward), lax.ppermute(first, axes, backward)
 
 
 def pack_kernel(slot_ref, code_ref, rows_ref, out_rows, out_codes, rows_wide, packed):
@@ -193,15 +193,9 @@
 CHUNK = 288
 
 
-def fill_padded(padded, low_ref, block_ref, high_ref):
-    rows, columns = block_ref.shape[0], block_ref.shape[1]
-    for row in range(rows + 2):
-        if row == 0:
-            source, at = low_ref, 0
-        elif row == rows + 1:
-            source, at = high_ref, 0
-        else:
-            source, at = block_ref, row - 1
+def fill_padded(padded, sources):
+    for row, (source, at) in enumerate(sources):
+        columns = source.shape[1]
         padded[row, HALO : HALO + columns, :] = source[at]
         padded[row, 0:HALO, :] = source[at, columns - HALO : columns, :]
         padded[row, HALO + columns : 2 * HALO + columns, :] = source[at, 0:HALO, :]
@@ -227,34 +221,31 @@
     return total
 
 
-def layer_kernel(
-    low_ref,
-    field_ref,
-    high_ref,
-    taps_ref,
-    in_ref,
-    out_ref,
-    in_t_ref,
-    out_t_ref,
-    cot_ref,
-    grid_ref,
-    grad_ref,
-    padded,
-):
-    fill_padded(padded, low_ref, field_ref, high_ref)
-    rows, columns = field_ref.shape[0], field_ref.shape[1]
+def layer_kernel(edge, *refs):
+    if edge:
+        low_ref, high_ref, *refs = refs
+    field_ref, taps_ref, in_ref, out_ref, in_t_ref, out_t_ref, cot_ref, *refs = refs
+    grid_ref, grad_ref, padded = refs
+    lat_rows, columns = field_ref.shape[0], field_ref.shape[1]
+    inside = [(field_ref, row) for row in range(lat_rows)]
+    if edge:
+        fill_padded(padded, [(low_ref, 0)] + inside[:2] + inside[-2:] + [(high_ref, 0)])
+    else:
+        fill_padded(padded, inside)
+    rows = grid_ref.shape[0]
     pieces = columns // CHUNK
 
     @pl.loop(0, rows * pieces)
     def _(index):
         row = index // pieces
+        band_row = row * (lat_rows - 1) if edge else row + 1
         start = pl.multiple_of((index % pieces) * CHUNK, 32)
         at = pl.ds(start, CHUNK)
-        mixed = stencil(padded, taps_ref, row, start, 1)
+        mixed = stencil(padded, taps_ref, 3 * row if edge else row, start, 1)
         inverse = lax.rsqrt(jnp.mean(mixed * mixed, axis=1, keepdims=True) + 1e-06)
         normed = (mixed * inverse).astype(jnp.bfloat16)
         inner = jnp.dot(normed, in_ref[...], preferred_element_type=jnp.float32)
-        cot = cot_ref[row, at, :]
+        cot = cot_ref[band_row, at, :]
         grad_hidden = jnp.dot(cot, out_t_ref[...], preferred_element_type=jnp.float32)
         grad_hidden = grad_hidden.astype(jnp.bfloat16).astype(jnp.float32)
         scale = 0.7978845608028654
@@ -265,7 +256,7 @@
         slope = (2.0 * scale) + (6.0 * scale * 0.044715) * square
         grad_inner = grad_hidden * (half + inner * (half - half * half) * slope)
         result = jnp.dot(hidden, out_ref[...], preferred_element_type=jnp.float32)
-        grid_ref[row, at, :] = (field_ref[row, at, :].astype(jnp.float32) + result).astype(
+        grid_ref[row, at, :] = (field_ref[band_row, at, :].astype(jnp.float32) + result).astype(
             jnp.bfloat16
         )
         grad_normed = jnp.dot(
@@ -277,49 +268,81 @@
         grad_ref[row, at, :] = grad_mixed.astype(jnp.bfloat16)
 
 
-def layer(edges, field, taps, weight_in, weight_out, cotangent):
-    rows, columns, width = field.shape
+def layer(edges, field, taps, weights, cotangent):
+    lat_rows, columns, width = field.shape
+    edge = len(edges) > 0
+    rows = 2 if edge else lat_rows - 2
     vmem = pl.BlockSpec(memory_space=pltpu.VMEM)
-    shape = jax.ShapeDtypeStruct(field.shape, jnp.bfloat16)
+    shape = jax.ShapeDtypeStruct((rows, columns, width), jnp.bfloat16)
+    depth = 6 if edge else lat_rows
     return pl.pallas_call(
-        layer_kernel,
+        functools.partial(layer_kernel, edge),
         out_shape=(shape, shape),
-        in_specs=[vmem] * 9,
+        in_specs=[vmem] * (len(edges) + 7),
         out_specs=(vmem, vmem),
-        scratch_shapes=[pltpu.VMEM((rows + 2, columns + 2 * HALO, width), jnp.bfloat16)],
-        compiler_params=pltpu.CompilerParams(vmem_limit_bytes=40 << 20),
-    )(edges[0], field, edges[1], taps, weight_in, weight_out, weight_in.T, weight_out.T, cotangent)
-
-
-def back_kernel(low_ref, grad_ref, high_ref, taps_ref, cot_ref, density_ref, cells_ref, padded):
-    fill_padded(padded, low_ref, grad_ref, high_ref)
-    rows, columns = grad_ref.shape[0], grad_ref.shape[1]
+        scratch_shapes=[pltpu.VMEM((depth, columns + 2 * HALO, width), jnp.bfloat16)],
+        cost_estimate=pl.CostEstimate(
+            flops=8 * rows * columns * weights[0].size,
+            bytes_accessed=8 * rows * columns * width,
+            transcendentals=rows * columns * weights[0].shape[1],
+        ),
+        compiler_params=pltpu.CompilerParams(vmem_limit_bytes=36 << 20),
+    )(*edges, field, taps, *weights, cotangent)
+
+
+def back_kernel(edge, *refs):
+    if edge:
+        low_ref, high_ref, *refs = refs
+    edge_ref, mid_ref, taps_ref, cot_ref, density_ref, cells_ref, padded = refs
+    lat_rows, columns = cot_ref.shape[0], cot_ref.shape[1]
+    inside = [(edge_ref, 0)] + [(mid_ref, row) for row in range(lat_rows - 2)] + [(edge_ref, 1)]
+    if edge:
+        fill_padded(padded, [(low_ref, 0)] + inside[:2] + inside[-2:] + [(high_ref, 0)])
+    else:
+        fill_padded(padded, inside)
+    rows = cells_ref.shape[0] // columns
     pieces = columns // CHUNK
 
     @pl.loop(0, rows * pieces)
     def _(index):
         row = index // pieces
+        band_row = row * (lat_rows - 1) if edge else row + 1
         start = pl.multiple_of((index % pieces) * CHUNK, 32)
         at = pl.ds(start, CHUNK)
         cells = pl.ds(pl.multiple_of(index * CHUNK, 32), CHUNK)
-        grad = stencil(padded, taps_ref, row, start, -1)
-        grad = cot_ref[row, at, :].astype(jnp.float32) + grad
-        density = density_ref[cells, :]
+        held = pl.ds(pl.multiple_of(band_row * columns + start, 32), CHUNK)
+        grad = stencil(padded, taps_ref, 3 * row if edge else row, start, -1)
+        grad = cot_ref[band_row, at, :].astype(jnp.float32) + grad
+        density = density_ref[held, :]
         density = jnp.concatenate([density] * (grad.shape[1] // density.shape[1]), axis=1)
         cells_ref[cells, :] = (grad / density).astype(jnp.bfloat16)
 
 
-def back(edges, grad_mixed, taps, cotangent, density):
-    rows, columns, width = grad_mixed.shape
+def back(edges, grad_edge, grad_mid, taps, cotangent, density):
+    lat_rows, columns, width = cotangent.shape
+    edge = len(edges) > 0
+    rows = 2 if edge else lat_rows - 2
     vmem = pl.BlockSpec(memory_space=pltpu.VMEM)
+    depth = 6 if edge else lat_rows
     return pl.pallas_call(
-        back_kernel,
+        functools.partial(back_kernel, edge),
         out_shape=jax.ShapeDtypeStruct((rows * columns, width), jnp.bfloat16),
-        in_specs=[vmem] * 6,
+        in_specs=[vmem] * (len(edges) + 5),
         out_specs=vmem,
-        scratch_shapes=[pltpu.VMEM((rows + 2, columns + 2 * HALO, width), jnp.bfloat16)],
-        compiler_params=pltpu.CompilerParams(vmem_limit_bytes=40 << 20),
-    )(edges[0], grad_mixed, edges[1], taps, cotangent, density)
+        scratch_shapes=[pltpu.VMEM((depth, columns + 2 * HALO, width), jnp.bfloat16)],
+        cost_estimate=pl.CostEstimate(
+            flops=40 * rows * columns * width,
+            bytes_accessed=10 * rows * columns * width,
+            transcendentals=0,
+        ),
+        compiler_params=pltpu.CompilerParams(vmem_limit_bytes=36 << 20),
+    )(*edges, grad_edge, grad_mid, taps, cotangent, density)
+
+
+def outer_sum(sums, cells):
+    return lax.dot_general(
+        sums, cells, (((0,), (0,)), ((), ())), preferred_element_type=jnp.float32
+    )
 
 
 def on_device(
@@ -404,16 +427,17 @@
         pitch,
     )
     field = field.reshape(lat_rows, lon_cells, width)
-    grid_output, grad_mixed = layer(
-        edge_rows(field), field, stencil_taps, weight_in, weight_out, grid_cotangent
-    )
-    grad_cells = back(edge_rows(grad_mixed), grad_mixed, stencil_taps, grid_cotangent, density)
-    local_grad = lax.dot_general(
-        sums,
-        grad_cells,
-        (((0,), (0,)), ((), ())),
-        preferred_element_type=jnp.float32,
-    )
+    matrices = (weight_in, weight_out, weight_in.T, weight_out.T)
+    edges = edge_rows(field[:1], field[-1:])
+    mid_output, mid_grad = layer((), field, stencil_taps, matrices, grid_cotangent)
+    edge_output, edge_grad = layer(edges, field, stencil_taps, matrices, grid_cotangent)
+    grad_edges = edge_rows(edge_grad[:1], edge_grad[1:])
+    grid_output = jnp.concatenate([edge_output[:1], mid_output, edge_output[1:]], axis=0)
+    mid_cells = back((), edge_grad, mid_grad, stencil_taps, grid_cotangent, density)
+    local_grad = outer_sum(sums[lon_cells : band_cells - lon_cells], mid_cells)
+    edge_cells = back(grad_edges, edge_grad, mid_grad, stencil_taps, grid_cotangent, density)
+    local_grad = local_grad + outer_sum(sums[:lon_cells], edge_cells[:lon_cells])
+    local_grad = local_grad + outer_sum(sums[band_cells - lon_cells :], edge_cells[lon_cells:])
     tiles = peer_count // 2
     shares = local_grad.astype(jnp.bfloat16).reshape(2, tiles, -1, width)
     shares = lax.all_to_all(

time: 245 us -> 231 us (0.943); the launches traced: 241 us -> 230 us
  waiting for transfers between devices: 55.7 us -> 50.9 us
  Pallas kernels: 88.4 us -> 84.6 us
  blocking collectives: 40 us -> 36.8 us
    all_to_all x1, blocking collectives: 40 us -> 36.8 us  [on_device(): lax.all_to_all(jnp.swapaxes(shares, 0, 1).reshape(peer_count, -1, width),...]
    ppermute x4, waiting for transfers between devices: 2.89 us -> 0.1 us  [the longest x2 0.09 us: edge_rows(): lax.ppermute(first, axes, backward)]
    pallas_call x1, Pallas kernels: 37.3 us -> 34.7 us  [deposit_cells(): pl.pallas_call(functools.partial(deposit_kernel, instr_dev, capacity, pit...]
    pallas_call x2 -> x4, Pallas kernels: 40.7 us -> 39.6 us  [the longest x2 33.3 us: layer(): pl.pallas_call(functools.partial(layer_kernel, edge), out_shape=(shape, s...]
    dot_general x1 -> x3, matrix products: 6.4 us -> 5.86 us  [outer_sum(): lax.dot_general(sums, cells, (((0,), (0,)), ((), ())), preferred_element_...]
    unnamed x32 -> x54, local copies, waits for them, and re-layouts: 8.07 us -> 8.15 us
  transfers between devices with their start and end apart: 9 -> 9, of which waited for: 8 -> 6; matrix products, arithmetic and copies ran while one was open for 2% -> 3% of each run, Pallas kernels for 0% -> 8%
where the time goes in v3:
time: 231 us; the launch traced here: 230 us
  Pallas kernels  84.6 us (37%)
  waiting for transfers between devices  50.9 us (22%)
  blocking collectives  36.8 us (16%)
  starting transfers between devices  23.5 us (10%)
  other arithmetic  15 us (6%)
  local copies, waits for them, and re-layouts  12.4 us (5%)
  matrix products  5.86 us (3%)
    all_to_all x1, waiting for transfers between devices, on_device(): lax.all_to_all(jnp.concatenate([send_rows.reshape(peer_count, capacity, f...  39.7 us
    all_to_all x1, blocking collectives, on_device(): lax.all_to_all(jnp.swapaxes(shares, 0, 1).reshape(peer_count, -1, width),...  36.8 us
    pallas_call x1, Pallas kernels, deposit_cells(): pl.pallas_call(functools.partial(deposit_kernel, instr_dev, capacity, pit...  34.7 us
    pallas_call x2, Pallas kernels, layer(): pl.pallas_call(functools.partial(layer_kernel, edge), out_shape=(shape, s...  33.3 us
    pallas_call x1, Pallas kernels, pack(): pl.pallas_call(pack_kernel, out_shape=(jax.ShapeDtypeStruct((slot_total,...  10.3 us
    ppermute x3, waiting for transfers between devices, gathered_over_tile(): lax.ppermute(block, 'tile', [(i, i ^ distance) for i in range(count)])  9.9 us
    ppermute x2, starting transfers between devices, edge_rows(): lax.ppermute(last, axes, forward)  9.47 us
    unnamed x54, local copies, waits for them, and re-layouts  8.15 us
  transfers between devices with their start and end apart: 9, of which 6 were waited for; matrix products, arithmetic and copies ran while one was open for 3% of the time, Pallas kernels for 8%

profile of v3, /device:TPU:0, one launch (start us, length us, event | category | flops | bytes accessed | tf_op | source)
XLA Modules:
  0.0 230.1 jit_solution(16941781893229282679)
XLA Ops:
  1.4 4.6 %reduce-window.6 = s32[16,32,128]{2,1,0:T(8,128)S(1)} reduce-window(s32[16,32,128]{2,1,0:T(8,128)S(1)} %fusion.17, s32[]{:T(128)} %constant.68.clone.1), window={size=1x1x128 pad=0_0x0_0x127_0}, to_apply=%region_0.1 | reduce-window | flops 8323072 | bytes 524292 | tf_op jit(solution)/shard_map/reduce-window
  7.5 1.4 select_reduce_fusion
  9.1 10.3 %shard_map.113 = (bf16[8192,128]{1,0:T(8,128)(2,1)S(1)}, s32[8192]{0:T(1024)S(1)}) custom-call(s32[4096]{0:T(1024)S(1)} %get-tuple-element.37.slot_ref, s32[4096]{0:T(1024)S(1)} %get-tuple-element.36.code_ref, bf16[4096,128]{1,0:T(8,128)(2,1)S(1)} %copy-done.6), custom_call_target="tpu_custom_call" | custom-call | tf_op jit(solution)/shard_map/pallas_call | solution.py:54
  19.6 1.9 maximum_maximum_fusion
  21.4 7.5 %all-to-all-start = ((bf16[16,528,128]{2,1,0:T(8,128)(2,1)}), bf16[16,528,128]{2,1,0:T(8,128)(2,1)S(1)}, u32[]{:S(2)}, u32[]{:S(2)}) async-start(bf16[16,528,128]{2,1,0:T(8,128)(2,1)} %maximum_maximum_fusion), calls=%async_computation | async-start | bytes 4325376 | tf_op jit(solution)/shard_map/all_to_all | solution.py:402
  29.4 1.2 collective-permute-done
  31.5 39.7 %all-to-all-done = bf16[16,528,128]{2,1,0:T(8,128)(2,1)S(1)} async-done(((bf16[16,528,128]{2,1,0:T(8,128)(2,1)}), bf16[16,528,128]{2,1,0:T(8,128)(2,1)S(1)}, u32[]{:S(2)}, u32[]{:S(2)}) %all-to-all-start) | async-done | bytes 2162720 | tf_op jit(solution)/shard_map/all_to_all | solution.py:402
  73.3 34.7 %shard_map.114 = (bf16[5760,1024]{1,0:T(8,128)(2,1)}, bf16[5760,256]{1,0:T(8,128)(2,1)}, f32[5760,128]{1,0:T(8,128)}) custom-call(s32[8192]{0:T(1024)} %bitcast.60, s32[8192]{0:T(1024)} %fusion.20.cell_ref, s32[8]{0:T(128)} %and_select_fusion.bound_ref, bf16[8448,128]{1,0:T(8,128)(2,1)} %bitcast.53, bf16[1024,256]{1,0:T(8,128)(2,1)} %bitcast.56, ...), custom_call_target="tpu_custom_call" | custom-call | tf_op jit(solution)/shard_map/pallas_call | solution.py:161
  108.0 2.7 %slice_bitcast_fusion = (bf16[1,1440,256]{2,1,0:T(8,128)(2,1)}, bf16[1,1440,256]{2,1,0:T(8,128)(2,1)}) fusion(bf16[5760,256]{1,0:T(8,128)(2,1)} %get-tuple-element.13), kind=kLoop, calls=%fused_computation.15 | loop fusion | bytes 2949120 | tf_op jit(solution)/shard_map/slice | solution.py:431
  110.7 2.2 collective-permute-start.1
  112.9 1.3 collective-permute-start.2
  114.2 1.0 copy.18
  115.2 2.0 copy.19
  117.3 1.8 copy-done.7
  119.2 1.0 copy-done.10
  120.2 1.0 copy-done.12
  121.2 1.0 copy-done.14
  122.3 17.4 %shard_map.115 = (bf16[2,1440,256]{2,1,0:T(8,128)(2,1)S(1)}, bf16[2,1440,256]{2,1,0:T(8,128)(2,1)S(1)}) custom-call(bf16[1,1440,256]{2,1,0:T(8,128)(2,1)} %collective-permute-done.1.refs_0_, bf16[1,1440,256]{2,1,0:T(8,128)(2,1)} %collective-permute-done.2.refs_1_, bf16[4,1440,256]{2,1,0:T(8,128)(2,1)S(1)} %bitcast.46, f32[9,256]{1,0:T(8,128)S(1)} %copy-done.16, ...), custom_call_target="tpu_custom_call" | custom-call | flops 6039797760 | bytes 5898240 | tf_op jit(solution)/shard_map/pallas_call | solution.py:278
  139.8 7.3 %collective-permute-start.3 = (bf16[1,1440,256]{2,1,0:T(8,128)(2,1)S(1)}, bf16[1,1440,256]{2,1,0:T(8,128)(2,1)S(1)}, u32[]{:S(2)}, u32[]{:S(2)}) collective-permute-start(bf16[1,1440,256]{2,1,0:T(8,128)(2,1)S(1)} %get-tuple-element.25), channel_id=1, source_target_pairs={{0,1},{1,2},{2,3},{3,4},{4,5},{5,6},{6,7},{7,8},{8,9},{9,10},{10,1... | collective-permute-start | bytes 2211848 | tf_op jit(solution)/shard_map/ppermute | solution.py:16
  147.2 1.7 collective-permute-start.4
  149.0 15.9 %shard_map.116 = (bf16[2,1440,256]{2,1,0:T(8,128)(2,1)S(1)}, bf16[2,1440,256]{2,1,0:T(8,128)(2,1)S(1)}) custom-call(bf16[4,1440,256]{2,1,0:T(8,128)(2,1)S(1)} %bitcast.47, f32[9,256]{1,0:T(8,128)S(1)} %copy-done.16, bf16[256,1024]{1,0:T(8,128)(2,1)S(1)} %copy-done.9, bf16[1024,256]{1,0:T(8,128)(2,1)S(1)} %copy-done.11, bf16[1024,256]{1,0:T(8,128)(2,1)S(1)} %bitcast.49, ...), custom_call_target="tpu_custom_call" | custom-call | flops 6039797760 | bytes 5898240 | tf_op jit(solution)/shard_map/pallas_call | solution.py:278
  164.9 3.1 %shard_map.117 = bf16[2880,256]{1,0:T(8,128)(2,1)S(1)} custom-call(bf16[2,1440,256]{2,1,0:T(8,128)(2,1)S(1)} %get-tuple-element.17.refs_0_.refs_2_, bf16[2,1440,256]{2,1,0:T(8,128)(2,1)S(1)} %get-tuple-element.18.refs_1_.refs_3_, f32[9,256]{1,0:T(8,128)S(1)} %copy-done.16, bf16[4,1440,256]{2,1,0:T(8,128)(2,1)S(1)} %copy-done, f32[5760,128]{1,0:T(8,128)S(1)} %copy-done.1), custom_call_target="tpu_custom_call" | custom-call | flops 29491200 | bytes 7372800 | tf_op jit(solution)/shard_map/pallas_call | solution.py:327
  168.1 3.2 %shard_map.118 = bf16[2880,256]{1,0:T(8,128)(2,1)S(1)} custom-call(bf16[1,1440,256]{2,1,0:T(8,128)(2,1)S(1)} %collective-permute-done.3.refs_0_, bf16[1,1440,256]{2,1,0:T(8,128)(2,1)S(1)} %collective-permute-done.4.refs_1_, bf16[2,1440,256]{2,1,0:T(8,128)(2,1)S(1)} %get-tuple-element.17.refs_0_.refs_2_, ...), custom_call_target="tpu_custom_call" | custom-call | flops 29491200 | bytes 7372800 | tf_op jit(solution)/shard_map/pallas_call | solution.py:327
  171.3 3.0 %fusion.2 = f32[1024,256]{1,0:T(8,128)S(1)} fusion(bf16[5760,1024]{1,0:T(8,128)(2,1)} %get-tuple-element.16, bf16[2880,256]{1,0:T(8,128)(2,1)S(1)} %shard_map.118), kind=kOutput, calls=%fused_computation.3 | convolution fusion | flops 754974720 | bytes 4734976 | tf_op jit(solution)/shard_map/dot_general | solution.py:343
  174.3 1.0 fusion.4
  175.4 1.8 fusion.12
  177.3 36.8 %all_to_all.10 = bf16[16,64,256]{2,1,0:T(8,128)(2,1)S(1)} all-to-all(bf16[16,64,256]{2,1,0:T(8,128)(2,1)S(1)} %bitcast.55), channel_id=1, replica_groups=mesh['parts'=2,'tile'=8,'stream'=2] {'tile','stream'}, dimensions={0} | all-to-all | bytes 1048576 | tf_op jit(solution)/shard_map/all_to_all | solution.py:443
  214.1 2.3 %collective-permute-start.5 = (bf16[64,256]{1,0:T(8,128)(2,1)S(1)}, bf16[64,256]{1,0:T(8,128)(2,1)S(1)}, u32[]{:S(2)}, u32[]{:S(2)}) collective-permute-start(bf16[64,256]{1,0:T(8,128)(2,1)S(1)} %reduce_sum.32), channel_id=1, source_target_pairs={{0,8},{2,10},{4,12},{6,14},{8,0},{10,2},{12,4},{14,6},{1,9},{3,11}... | collective-permute-start | bytes 98312 | tf_op jit(solution)/shard_map/ppermute | solution.py:182
  216.5 3.3 %collective-permute-done.5 = bf16[64,256]{1,0:T(8,128)(2,1)S(1)} collective-permute-done((bf16[64,256]{1,0:T(8,128)(2,1)S(1)}, bf16[64,256]{1,0:T(8,128)(2,1)S(1)}, u32[]{:S(2)}, u32[]{:S(2)}) %collective-permute-start.5) | collective-permute-done | bytes 32800 | tf_op jit(solution)/shard_map/ppermute | solution.py:182
  220.5 3.6 %collective-permute-done.6 = bf16[2,64,256]{2,1,0:T(8,128)(2,1)S(1)} collective-permute-done((bf16[2,64,256]{2,1,0:T(8,128)(2,1)S(1)}, bf16[2,64,256]{2,1,0:T(8,128)(2,1)S(1)}, u32[]{:S(2)}, u32[]{:S(2)}) %collective-permute-start.6) | collective-permute-done | bytes 65568 | tf_op jit(solution)/shard_map/ppermute | solution.py:182
  224.2 1.9 pad_maximum_fusion
  226.1 3.0 %collective-permute-done.7 = bf16[2,2,64,256]{3,2,1,0:T(8,128)(2,1)S(1)} collective-permute-done((bf16[2,2,64,256]{3,2,1,0:T(8,128)(2,1)S(1)}, bf16[2,2,64,256]{3,2,1,0:T(8,128)(2,1)S(1)}, u32[]{:S(2)}, u32[]{:S(2)}) %collective-permute-start.7) | collective-permute-done | bytes 131104 | tf_op jit(solution)/shard_map/ppermute | solution.py:182
  (85 shorter events, 8.0 us)
Async XLA Ops:
  0.6 6.9 %copy-start.20 = (s32[4096,1]{0,1:T(1,128)S(1)}, s32[4096,1]{0,1:T(1,128)}, u32[]{:S(2)}) copy-start(s32[4096,1]{0,1:T(1,128)} %param.12) | copy-start | bytes 49156
  6.9 2.2 copy-start.21
  6.9 2.2 copy-start.22
  6.9 2.2 copy-start.6
  21.4 7.5 %copy-start.19 = (bf16[4,128,256]{2,1,0:T(8,128)(2,1)S(1)}, bf16[4,128,256]{2,1,0:T(8,128)(2,1)}, u32[]{:S(2)}) copy-start(bf16[4,128,256]{2,1,0:T(8,128)(2,1)} %param.14) | copy-start | bytes 786436
  21.4 49.8 %all-to-all-start = ((bf16[16,528,128]{2,1,0:T(8,128)(2,1)}), bf16[16,528,128]{2,1,0:T(8,128)(2,1)S(1)}, u32[]{:S(2)}, u32[]{:S(2)}) async-start(bf16[16,528,128]{2,1,0:T(8,128)(2,1)} %maximum_maximum_fusion), calls=%async_computation | async-start | bytes 4325376 | tf_op jit(solution)/shard_map/all_to_all | solution.py:402
  29.0 1.6 collective-permute-start
  71.2 2.1 copy-start.17
  71.6 1.7 copy-start.18
  108.0 6.2 %copy-start.9 = (bf16[256,1024]{1,0:T(8,128)(2,1)S(1)}, bf16[256,1024]{1,0:T(8,128)(2,1)}, u32[]{:S(2)}) copy-start(bf16[256,1024]{1,0:T(8,128)(2,1)} %refs_2_.2) | copy-start | bytes 1572868
  108.0 9.4 %copy-start = (bf16[4,1440,256]{2,1,0:T(8,128)(2,1)S(1)}, bf16[4,1440,256]{2,1,0:T(8,128)(2,1)}, u32[]{:S(2)}) copy-start(bf16[4,1440,256]{2,1,0:T(8,128)(2,1)} %refs_5_.3) | copy-start | bytes 8847364
  108.0 9.4 %copy-start.16 = (f32[9,256]{1,0:T(8,128)S(1)}, f32[9,256]{1,0:T(8,128)}, u32[]{:S(2)}) copy-start(f32[9,256]{1,0:T(8,128)} %refs_4_.3) | copy-start | bytes 27652
  110.7 6.5 %collective-permute-start.1 = (bf16[1,1440,256]{2,1,0:T(8,128)(2,1)}, bf16[1,1440,256]{2,1,0:T(8,128)(2,1)}, u32[]{:S(2)}, u32[]{:S(2)}) collective-permute-start(bf16[1,1440,256]{2,1,0:T(8,128)(2,1)} %get-tuple-element.23), channel_id=1, source_target_pairs={{0,1},{1,2},{2,3},{3,4},{4,5},{5,6},{6,7},{7,8},{8,9},{9,10},{10,1... | collective-permute-start | bytes 2211848 | tf_op jit(solution)/shard_map/ppermute | solution.py:16
  112.9 4.4 %collective-permute-start.2 = (bf16[1,1440,256]{2,1,0:T(8,128)(2,1)}, bf16[1,1440,256]{2,1,0:T(8,128)(2,1)}, u32[]{:S(2)}, u32[]{:S(2)}) collective-permute-start(bf16[1,1440,256]{2,1,0:T(8,128)(2,1)} %get-tuple-element.22), channel_id=1, source_target_pairs={{1,0},{2,1},{3,2},{4,3},{5,4},{6,5},{7,6},{8,7},{9,8},{10,9},{11,1... | collective-permute-start | bytes 2211848 | tf_op jit(solution)/shard_map/ppermute | solution.py:16
  117.3 1.8 copy-start.7
  122.3 26.6 %copy-start.11 = (bf16[1024,256]{1,0:T(8,128)(2,1)S(1)}, bf16[1024,256]{1,0:T(8,128)(2,1)}, u32[]{:S(2)}) copy-start(bf16[1024,256]{1,0:T(8,128)(2,1)} %refs_3_.4) | copy-start | bytes 1572868
  122.3 26.6 %copy-start.13 = (bf16[256,1024]{0,1:T(8,128)(2,1)S(1)}, bf16[256,1024]{0,1:T(8,128)(2,1)}, u32[]{:S(2)}) copy-start(bf16[256,1024]{0,1:T(8,128)(2,1)} %copy.18) | copy-start | bytes 1572868
  122.3 26.6 %copy-start.15 = (bf16[1024,256]{0,1:T(8,128)(2,1)S(1)}, bf16[1024,256]{0,1:T(8,128)(2,1)}, u32[]{:S(2)}) copy-start(bf16[1024,256]{0,1:T(8,128)(2,1)} %copy.19) | copy-start | bytes 1572868
  139.7 7.4 %copy-start.4 = (bf16[2,1440,256]{2,1,0:T(8,128)(2,1)}, bf16[2,1440,256]{2,1,0:T(8,128)(2,1)S(1)}, u32[]{:S(2)}) copy-start(bf16[2,1440,256]{2,1,0:T(8,128)(2,1)S(1)} %get-tuple-element.14) | copy-start | bytes 4423684
  139.7 9.2 %copy-start.8 = (bf16[5760,256]{1,0:T(8,128)(2,1)S(1)}, bf16[5760,256]{1,0:T(8,128)(2,1)}, u32[]{:S(2)}) copy-start(bf16[5760,256]{1,0:T(8,128)(2,1)} %get-tuple-element.13) | copy-start | bytes 8847364
  139.8 28.2 %collective-permute-start.3 = (bf16[1,1440,256]{2,1,0:T(8,128)(2,1)S(1)}, bf16[1,1440,256]{2,1,0:T(8,128)(2,1)S(1)}, u32[]{:S(2)}, u32[]{:S(2)}) collective-permute-start(bf16[1,1440,256]{2,1,0:T(8,128)(2,1)S(1)} %get-tuple-element.25), channel_id=1, source_target_pairs={{0,1},{1,2},{2,3},{3,4},{4,5},{5,6},{6,7},{7,8},{8,9},{9,10},{10,1... | collective-permute-start | bytes 2211848 | tf_op jit(solution)/shard_map/ppermute | solution.py:16
  147.2 17.7 %copy-start.1 = (f32[5760,128]{1,0:T(8,128)S(1)}, f32[5760,128]{1,0:T(8,128)}, u32[]{:S(2)}) copy-start(f32[5760,128]{1,0:T(8,128)} %get-tuple-element.19.refs_4_.refs_6_) | copy-start | bytes 8847364
  147.2 20.9 %collective-permute-start.4 = (bf16[1,1440,256]{2,1,0:T(8,128)(2,1)S(1)}, bf16[1,1440,256]{2,1,0:T(8,128)(2,1)S(1)}, u32[]{:S(2)}, u32[]{:S(2)}) collective-permute-start(bf16[1,1440,256]{2,1,0:T(8,128)(2,1)S(1)} %get-tuple-element.24), channel_id=1, source_target_pairs={{1,0},{2,1},{3,2},{4,3},{5,4},{6,5},{7,6},{8,7},{9,8},{10,9},{11,1... | collective-permute-start | bytes 2211848 | tf_op jit(solution)/shard_map/ppermute | solution.py:16
  164.9 3.1 %copy-start.2 = (bf16[2,1440,256]{2,1,0:T(8,128)(2,1)}, bf16[2,1440,256]{2,1,0:T(8,128)(2,1)S(1)}, u32[]{:S(2)}) copy-start(bf16[2,1440,256]{2,1,0:T(8,128)(2,1)S(1)} %get-tuple-element.15) | copy-start | bytes 4423684
  168.0 6.2 %slice-start = ((s8[11796480]{0:T(1024)(128)(4,1)}), s8[3407872]{0:T(1024)(128)(4,1)S(1)}, s32[]{:S(2)}) async-start(s8[11796480]{0:T(1024)(128)(4,1)} %bitcast.66), calls=%async_computation.2 | async-start | bytes 6815744
  168.1 6.2 %slice-start.1 = ((s8[11796480]{0:T(1024)(128)(4,1)}), s8[4194304]{0:T(1024)(128)(4,1)S(1)}, s32[]{:S(2)}) async-start(s8[11796480]{0:T(1024)(128)(4,1)} %bitcast.66), calls=%async_computation.3 | async-start | bytes 8388608
  171.3 3.1 %slice-start.2 = ((s8[11796480]{0:T(1024)(128)(4,1)}), s8[4194304]{0:T(1024)(128)(4,1)S(1)}, s32[]{:S(2)}) async-start(s8[11796480]{0:T(1024)(128)(4,1)} %bitcast.66), calls=%async_computation.4 | async-start | bytes 8388608
  177.2 43.1 %copy-start.5 = (bf16[2,1440,256]{2,1,0:T(8,128)(2,1)S(1)}, bf16[2,1440,256]{2,1,0:T(8,128)(2,1)}, u32[]{:S(2)}) copy-start(bf16[2,1440,256]{2,1,0:T(8,128)(2,1)} %copy-done.4) | copy-start | bytes 4423684
  214.1 10.1 %copy-start.3 = (bf16[2,1440,256]{2,1,0:T(8,128)(2,1)S(1)}, bf16[2,1440,256]{2,1,0:T(8,128)(2,1)}, u32[]{:S(2)}) copy-start(bf16[2,1440,256]{2,1,0:T(8,128)(2,1)} %copy-done.2) | copy-start | bytes 4423684
  214.1 5.6 %collective-permute-start.5 = (bf16[64,256]{1,0:T(8,128)(2,1)S(1)}, bf16[64,256]{1,0:T(8,128)(2,1)S(1)}, u32[]{:S(2)}, u32[]{:S(2)}) collective-permute-start(bf16[64,256]{1,0:T(8,128)(2,1)S(1)} %reduce_sum.32), channel_id=1, source_target_pairs={{0,8},{2,10},{4,12},{6,14},{8,0},{10,2},{12,4},{14,6},{1,9},{3,11}... | collective-permute-start | bytes 98312 | tf_op jit(solution)/shard_map/ppermute | solution.py:182
  219.8 4.3 %collective-permute-start.6 = (bf16[2,64,256]{2,1,0:T(8,128)(2,1)S(1)}, bf16[2,64,256]{2,1,0:T(8,128)(2,1)S(1)}, u32[]{:S(2)}, u32[]{:S(2)}) collective-permute-start(bf16[2,64,256]{2,1,0:T(8,128)(2,1)S(1)} %pad_maximum_fusion.3), channel_id=1, source_target_pairs={{0,4},{2,6},{4,0},{6,2},{8,12},{10,14},{12,8},{14,10},{1,5},{3,7},... | collective-permute-start | bytes 196616 | tf_op jit(solution)/shard_map/ppermute | solution.py:182
  224.1 5.0 %collective-permute-start.7 = (bf16[2,2,64,256]{3,2,1,0:T(8,128)(2,1)S(1)}, bf16[2,2,64,256]{3,2,1,0:T(8,128)(2,1)S(1)}, u32[]{:S(2)}, u32[]{:S(2)}) collective-permute-start(bf16[2,2,64,256]{3,2,1,0:T(8,128)(2,1)S(1)} %pad_maximum_fusion.2), channel_id=1, source_target_pairs={{0,2},{2,0},{4,6},{6,4},{8,10},{10,8},{12,14},{14,12},{1,3},{3,1},... | collective-permute-start | bytes 393224 | tf_op jit(solution)/shard_map/ppermute | solution.py:182
  (3 other events, 3.1 us)

commit v4 on v3

--- a/solution.py
+++ b/solution.py
@@ -430,6 +430,7 @@
     matrices = (weight_in, weight_out, weight_in.T, weight_out.T)
     edges = edge_rows(field[:1], field[-1:])
     mid_output, mid_grad = layer((), field, stencil_taps, matrices, grid_cotangent)
+    edges, mid_grad = lax.optimization_barrier((edges, mid_grad))
     edge_output, edge_grad = layer(edges, field, stencil_taps, matrices, grid_cotangent)
     grad_edges = edge_rows(edge_grad[:1], edge_grad[1:])
     grid_output = jnp.concatenate([edge_output[:1], mid_output, edge_output[1:]], axis=0)

time: 231 us -> 231 us (level); the launches traced: 230 us -> 228 us
  Pallas kernels: 84.6 us -> 73.9 us
  starting transfers between devices: 23.5 us -> 33.4 us
    pallas_call x1, Pallas kernels: 34.7 us -> 24.2 us  [deposit_cells(): pl.pallas_call(functools.partial(deposit_kernel, instr_dev, capacity, pit...]
    ppermute x2, starting transfers between devices: 9.47 us -> 19.7 us  [edge_rows(): lax.ppermute(last, axes, forward)]
    unnamed x54 -> x48, local copies, waits for them, and re-layouts: 8.15 us -> 9.26 us
where the time goes in v4:
time: 231 us; the launch traced here: 228 us
  Pallas kernels  73.9 us (32%)
  waiting for transfers between devices  52.2 us (23%)
  blocking collectives  34.7 us (15%)
  starting transfers between devices  33.4 us (14%)
  other arithmetic  15 us (6%)
  local copies, waits for them, and re-layouts  13.5 us (6%)
  matrix products  3.89 us (2%)
    all_to_all x1, waiting for transfers between devices, on_device(): lax.all_to_all(jnp.concatenate([send_rows.reshape(peer_count, capacity, f...  39.7 us
    all_to_all x1, blocking collectives, on_device(): lax.all_to_all(jnp.swapaxes(shares, 0, 1).reshape(peer_count, -1, width),...  34.7 us
    pallas_call x2, Pallas kernels, layer(): pl.pallas_call(functools.partial(layer_kernel, edge), out_shape=(shape, s...  33.1 us
    pallas_call x1, Pallas kernels, deposit_cells(): pl.pallas_call(functools.partial(deposit_kernel, instr_dev, capacity, pit...  24.2 us
    ppermute x2, starting transfers between devices, edge_rows(): lax.ppermute(last, axes, forward)  19.7 us
    pallas_call x1, Pallas kernels, pack(): pl.pallas_call(pack_kernel, out_shape=(jax.ShapeDtypeStruct((slot_total,...  10.3 us
    ppermute x3, waiting for transfers between devices, gathered_over_tile(): lax.ppermute(block, 'tile', [(i, i ^ distance) for i in range(count)])  9.9 us
    unnamed x48, local copies, waits for them, and re-layouts  9.26 us
  transfers between devices with their start and end apart: 9, of which 6 were waited for; matrix products, arithmetic and copies ran while one was open for 3% of the time, Pallas kernels for 8%

profile of v4, /device:TPU:0, one launch (start us, length us, event | category | flops | bytes accessed | tf_op | source)
XLA Modules:
  0.0 227.7 jit_solution(9029960104704176253)
XLA Ops:
  1.4 4.6 %reduce-window.6 = s32[16,32,128]{2,1,0:T(8,128)S(1)} reduce-window(s32[16,32,128]{2,1,0:T(8,128)S(1)} %fusion.17, s32[]{:T(128)} %constant.68.clone.1), window={size=1x1x128 pad=0_0x0_0x127_0}, to_apply=%region_0.1 | reduce-window | flops 8323072 | bytes 524292 | tf_op jit(solution)/shard_map/reduce-window
  7.5 1.4 select_reduce_fusion
  9.1 10.3 %shard_map.113 = (bf16[8192,128]{1,0:T(8,128)(2,1)S(1)}, s32[8192]{0:T(1024)S(1)}) custom-call(s32[4096]{0:T(1024)S(1)} %get-tuple-element.43.slot_ref, s32[4096]{0:T(1024)S(1)} %get-tuple-element.42.code_ref, bf16[4096,128]{1,0:T(8,128)(2,1)S(1)} %copy-done.6), custom_call_target="tpu_custom_call" | custom-call | tf_op jit(solution)/shard_map/pallas_call | solution.py:54
  19.6 1.9 maximum_maximum_fusion
  21.4 7.5 %all-to-all-start = ((bf16[16,528,128]{2,1,0:T(8,128)(2,1)}), bf16[16,528,128]{2,1,0:T(8,128)(2,1)S(1)}, u32[]{:S(2)}, u32[]{:S(2)}) async-start(bf16[16,528,128]{2,1,0:T(8,128)(2,1)} %maximum_maximum_fusion), calls=%async_computation | async-start | bytes 4325376 | tf_op jit(solution)/shard_map/all_to_all | solution.py:402
  29.4 1.2 collective-permute-done
  31.5 39.7 %all-to-all-done = bf16[16,528,128]{2,1,0:T(8,128)(2,1)S(1)} async-done(((bf16[16,528,128]{2,1,0:T(8,128)(2,1)}), bf16[16,528,128]{2,1,0:T(8,128)(2,1)S(1)}, u32[]{:S(2)}, u32[]{:S(2)}) %all-to-all-start) | async-done | bytes 2162720 | tf_op jit(solution)/shard_map/all_to_all | solution.py:402
  73.3 24.2 %shard_map.114 = (bf16[5760,1024]{1,0:T(8,128)(2,1)}, bf16[5760,256]{1,0:T(8,128)(2,1)}, f32[5760,128]{1,0:T(8,128)}) custom-call(s32[8192]{0:T(1024)} %bitcast.60, s32[8192]{0:T(1024)} %fusion.20.cell_ref, s32[8]{0:T(128)} %and_select_fusion.bound_ref, bf16[8448,128]{1,0:T(8,128)(2,1)} %bitcast.53, bf16[1024,256]{1,0:T(8,128)(2,1)} %bitcast.56, ...), custom_call_target="tpu_custom_call" | custom-call | tf_op jit(solution)/shard_map/pallas_call | solution.py:161
  97.5 2.7 %slice_bitcast_fusion = (bf16[1,1440,256]{2,1,0:T(8,128)(2,1)}, bf16[1,1440,256]{2,1,0:T(8,128)(2,1)}) fusion(bf16[5760,256]{1,0:T(8,128)(2,1)} %get-tuple-element.16), kind=kLoop, calls=%fused_computation.15 | loop fusion | bytes 2949120 | tf_op jit(solution)/shard_map/slice | solution.py:431
  100.2 16.3 %collective-permute-start.1 = (bf16[1,1440,256]{2,1,0:T(8,128)(2,1)}, bf16[1,1440,256]{2,1,0:T(8,128)(2,1)}, u32[]{:S(2)}, u32[]{:S(2)}) collective-permute-start(bf16[1,1440,256]{2,1,0:T(8,128)(2,1)} %get-tuple-element.29), channel_id=1, source_target_pairs={{0,1},{1,2},{2,3},{3,4},{4,5},{5,6},{6,7},{7,8},{8,9},{9,10},{10,1... | collective-permute-start | bytes 2211848 | tf_op jit(solution)/shard_map/ppermute | solution.py:16
  116.6 1.3 collective-permute-start.2
  118.9 2.1 copy.19
  121.0 1.8 copy-done.7
  122.8 1.0 copy-done.10
  123.9 1.0 copy-done.11
  124.9 1.0 copy-done.12
  125.9 15.8 %shard_map.115 = (bf16[2,1440,256]{2,1,0:T(8,128)(2,1)S(1)}, bf16[2,1440,256]{2,1,0:T(8,128)(2,1)S(1)}) custom-call(bf16[4,1440,256]{2,1,0:T(8,128)(2,1)S(1)} %bitcast.46, f32[9,256]{1,0:T(8,128)S(1)} %copy-done.13, bf16[256,1024]{1,0:T(8,128)(2,1)S(1)} %copy-done.9, bf16[1024,256]{1,0:T(8,128)(2,1)S(1)} %copy-done.10, bf16[1024,256]{1,0:T(8,128)(2,1)S(1)} %bitcast.48, ...), custom_call_target="tpu_custom_call" | custom-call | flops 6039797760 | bytes 5898240 | tf_op jit(solution)/shard_map/pallas_call | solution.py:278
  141.7 1.1 copy-done.2
  142.9 17.4 %shard_map.116 = (bf16[2,1440,256]{2,1,0:T(8,128)(2,1)S(1)}, bf16[2,1440,256]{2,1,0:T(8,128)(2,1)S(1)}) custom-call(bf16[1,1440,256]{2,1,0:T(8,128)(2,1)} %collective-permute-done.1.refs_0_, bf16[1,1440,256]{2,1,0:T(8,128)(2,1)} %collective-permute-done.2.refs_1_, bf16[4,1440,256]{2,1,0:T(8,128)(2,1)S(1)} %bitcast.47, f32[9,256]{1,0:T(8,128)S(1)} %copy-done.13, ...), custom_call_target="tpu_custom_call" | custom-call | flops 6039797760 | bytes 5898240 | tf_op jit(solution)/shard_map/pallas_call | solution.py:278
  160.4 3.4 %collective-permute-start.3 = (bf16[1,1440,256]{2,1,0:T(8,128)(2,1)S(1)}, bf16[1,1440,256]{2,1,0:T(8,128)(2,1)S(1)}, u32[]{:S(2)}, u32[]{:S(2)}) collective-permute-start(bf16[1,1440,256]{2,1,0:T(8,128)(2,1)S(1)} %get-tuple-element.31), channel_id=1, source_target_pairs={{0,1},{1,2},{2,3},{3,4},{4,5},{5,6},{6,7},{7,8},{8,9},{9,10},{10,1... | collective-permute-start | bytes 2211848 | tf_op jit(solution)/shard_map/ppermute | solution.py:16
  163.7 1.5 collective-permute-start.4
  165.2 3.1 %shard_map.117 = bf16[2880,256]{1,0:T(8,128)(2,1)S(1)} custom-call(bf16[2,1440,256]{2,1,0:T(8,128)(2,1)S(1)} %get-tuple-element.23.refs_0_.refs_2_, bf16[2,1440,256]{2,1,0:T(8,128)(2,1)S(1)} %get-tuple-element.24.refs_1_.refs_3_, f32[9,256]{1,0:T(8,128)S(1)} %copy-done.13, bf16[4,1440,256]{2,1,0:T(8,128)(2,1)S(1)} %copy-done, f32[5760,128]{1,0:T(8,128)S(1)} %copy-done.1), custom_call_target="tpu_custom_call" | custom-call | flops 29491200 | bytes 7372800 | tf_op jit(solution)/shard_map/pallas_call | solution.py:327
  168.4 1.4 collective-permute-done.4.refs_1_
  169.8 3.2 %shard_map.118 = bf16[2880,256]{1,0:T(8,128)(2,1)S(1)} custom-call(bf16[1,1440,256]{2,1,0:T(8,128)(2,1)S(1)} %collective-permute-done.3.refs_0_, bf16[1,1440,256]{2,1,0:T(8,128)(2,1)S(1)} %collective-permute-done.4.refs_1_, bf16[2,1440,256]{2,1,0:T(8,128)(2,1)S(1)} %get-tuple-element.23.refs_0_.refs_2_, ...), custom_call_target="tpu_custom_call" | custom-call | flops 29491200 | bytes 7372800 | tf_op jit(solution)/shard_map/pallas_call | solution.py:327
  174.1 1.0 fusion.2
  175.1 1.9 fusion.12
  177.0 34.7 %all_to_all.10 = bf16[16,64,256]{2,1,0:T(8,128)(2,1)S(1)} all-to-all(bf16[16,64,256]{2,1,0:T(8,128)(2,1)S(1)} %bitcast.55), channel_id=1, replica_groups=mesh['parts'=2,'tile'=8,'stream'=2] {'tile','stream'}, dimensions={0} | all-to-all | bytes 1048576 | tf_op jit(solution)/shard_map/all_to_all | solution.py:444
  211.8 2.3 %collective-permute-start.5 = (bf16[64,256]{1,0:T(8,128)(2,1)S(1)}, bf16[64,256]{1,0:T(8,128)(2,1)S(1)}, u32[]{:S(2)}, u32[]{:S(2)}) collective-permute-start(bf16[64,256]{1,0:T(8,128)(2,1)S(1)} %reduce_sum.32), channel_id=1, source_target_pairs={{0,8},{2,10},{4,12},{6,14},{8,0},{10,2},{12,4},{14,6},{1,9},{3,11}... | collective-permute-start | bytes 98312 | tf_op jit(solution)/shard_map/ppermute | solution.py:182
  214.1 3.3 %collective-permute-done.5 = bf16[64,256]{1,0:T(8,128)(2,1)S(1)} collective-permute-done((bf16[64,256]{1,0:T(8,128)(2,1)S(1)}, bf16[64,256]{1,0:T(8,128)(2,1)S(1)}, u32[]{:S(2)}, u32[]{:S(2)}) %collective-permute-start.5) | collective-permute-done | bytes 32800 | tf_op jit(solution)/shard_map/ppermute | solution.py:182
  218.1 3.6 %collective-permute-done.6 = bf16[2,64,256]{2,1,0:T(8,128)(2,1)S(1)} collective-permute-done((bf16[2,64,256]{2,1,0:T(8,128)(2,1)S(1)}, bf16[2,64,256]{2,1,0:T(8,128)(2,1)S(1)}, u32[]{:S(2)}, u32[]{:S(2)}) %collective-permute-start.6) | collective-permute-done | bytes 65568 | tf_op jit(solution)/shard_map/ppermute | solution.py:182
  221.8 1.9 pad_maximum_fusion
  223.8 3.0 %collective-permute-done.7 = bf16[2,2,64,256]{3,2,1,0:T(8,128)(2,1)S(1)} collective-permute-done((bf16[2,2,64,256]{3,2,1,0:T(8,128)(2,1)S(1)}, bf16[2,2,64,256]{3,2,1,0:T(8,128)(2,1)S(1)}, u32[]{:S(2)}, u32[]{:S(2)}) %collective-permute-start.7) | collective-permute-done | bytes 131104 | tf_op jit(solution)/shard_map/ppermute | solution.py:182
  (79 shorter events, 9.9 us)
Async XLA Ops:
  0.6 6.9 %copy-start.17 = (s32[4096,1]{0,1:T(1,128)S(1)}, s32[4096,1]{0,1:T(1,128)}, u32[]{:S(2)}) copy-start(s32[4096,1]{0,1:T(1,128)} %param.12) | copy-start | bytes 49156
  6.9 2.2 copy-start.18
  6.9 2.2 copy-start.19
  6.9 2.2 copy-start.6
  21.4 7.5 %copy-start.16 = (bf16[4,128,256]{2,1,0:T(8,128)(2,1)S(1)}, bf16[4,128,256]{2,1,0:T(8,128)(2,1)}, u32[]{:S(2)}) copy-start(bf16[4,128,256]{2,1,0:T(8,128)(2,1)} %param.14) | copy-start | bytes 786436
  21.4 49.8 %all-to-all-start = ((bf16[16,528,128]{2,1,0:T(8,128)(2,1)}), bf16[16,528,128]{2,1,0:T(8,128)(2,1)S(1)}, u32[]{:S(2)}, u32[]{:S(2)}) async-start(bf16[16,528,128]{2,1,0:T(8,128)(2,1)} %maximum_maximum_fusion), calls=%async_computation | async-start | bytes 4325376 | tf_op jit(solution)/shard_map/all_to_all | solution.py:402
  29.0 1.6 collective-permute-start
  71.2 2.1 copy-start.14
  71.6 1.7 copy-start.15
  97.5 20.4 %copy-start.9 = (bf16[256,1024]{1,0:T(8,128)(2,1)S(1)}, bf16[256,1024]{1,0:T(8,128)(2,1)}, u32[]{:S(2)}) copy-start(bf16[256,1024]{1,0:T(8,128)(2,1)} %refs_4_.2) | copy-start | bytes 1572868
  97.5 23.4 %copy-start = (bf16[4,1440,256]{2,1,0:T(8,128)(2,1)S(1)}, bf16[4,1440,256]{2,1,0:T(8,128)(2,1)}, u32[]{:S(2)}) copy-start(bf16[4,1440,256]{2,1,0:T(8,128)(2,1)} %refs_5_.3) | copy-start | bytes 8847364
  97.5 23.5 %copy-start.13 = (f32[9,256]{1,0:T(8,128)S(1)}, f32[9,256]{1,0:T(8,128)}, u32[]{:S(2)}) copy-start(f32[9,256]{1,0:T(8,128)} %refs_4_.3) | copy-start | bytes 27652
  100.2 42.6 %collective-permute-start.1 = (bf16[1,1440,256]{2,1,0:T(8,128)(2,1)}, bf16[1,1440,256]{2,1,0:T(8,128)(2,1)}, u32[]{:S(2)}, u32[]{:S(2)}) collective-permute-start(bf16[1,1440,256]{2,1,0:T(8,128)(2,1)} %get-tuple-element.29), channel_id=1, source_target_pairs={{0,1},{1,2},{2,3},{3,4},{4,5},{5,6},{6,7},{7,8},{8,9},{9,10},{10,1... | collective-permute-start | bytes 2211848 | tf_op jit(solution)/shard_map/ppermute | solution.py:16
  116.6 26.3 %collective-permute-start.2 = (bf16[1,1440,256]{2,1,0:T(8,128)(2,1)}, bf16[1,1440,256]{2,1,0:T(8,128)(2,1)}, u32[]{:S(2)}, u32[]{:S(2)}) collective-permute-start(bf16[1,1440,256]{2,1,0:T(8,128)(2,1)} %get-tuple-element.28), channel_id=1, source_target_pairs={{1,0},{2,1},{3,2},{4,3},{5,4},{6,5},{7,6},{8,7},{9,8},{10,9},{11,1... | collective-permute-start | bytes 2211848 | tf_op jit(solution)/shard_map/ppermute | solution.py:16
  121.0 1.8 copy-start.7
  122.8 1.0 copy-start.10
  123.8 1.0 copy-start.11
  124.9 1.0 copy-start.12
  125.9 16.9 %copy-start.8 = (bf16[5760,256]{1,0:T(8,128)(2,1)S(1)}, bf16[5760,256]{1,0:T(8,128)(2,1)}, u32[]{:S(2)}) copy-start(bf16[5760,256]{1,0:T(8,128)(2,1)} %get-tuple-element.16) | copy-start | bytes 8847364
  141.7 1.2 copy-start.2
  160.2 8.1 %copy-start.4 = (bf16[2,1440,256]{2,1,0:T(8,128)(2,1)}, bf16[2,1440,256]{2,1,0:T(8,128)(2,1)S(1)}, u32[]{:S(2)}) copy-start(bf16[2,1440,256]{2,1,0:T(8,128)(2,1)S(1)} %get-tuple-element.20) | copy-start | bytes 4423684
  160.3 5.0 %copy-start.1 = (f32[5760,128]{1,0:T(8,128)S(1)}, f32[5760,128]{1,0:T(8,128)}, u32[]{:S(2)}) copy-start(f32[5760,128]{1,0:T(8,128)} %get-tuple-element.25.refs_4_.refs_6_) | copy-start | bytes 8847364
  160.4 8.0 %collective-permute-start.3 = (bf16[1,1440,256]{2,1,0:T(8,128)(2,1)S(1)}, bf16[1,1440,256]{2,1,0:T(8,128)(2,1)S(1)}, u32[]{:S(2)}, u32[]{:S(2)}) collective-permute-start(bf16[1,1440,256]{2,1,0:T(8,128)(2,1)S(1)} %get-tuple-element.31), channel_id=1, source_target_pairs={{0,1},{1,2},{2,3},{3,4},{4,5},{5,6},{6,7},{7,8},{8,9},{9,10},{10,1... | collective-permute-start | bytes 2211848 | tf_op jit(solution)/shard_map/ppermute | solution.py:16
  163.7 6.1 %collective-permute-start.4 = (bf16[1,1440,256]{2,1,0:T(8,128)(2,1)S(1)}, bf16[1,1440,256]{2,1,0:T(8,128)(2,1)S(1)}, u32[]{:S(2)}, u32[]{:S(2)}) collective-permute-start(bf16[1,1440,256]{2,1,0:T(8,128)(2,1)S(1)} %get-tuple-element.30), channel_id=1, source_target_pairs={{1,0},{2,1},{3,2},{4,3},{5,4},{6,5},{7,6},{8,7},{9,8},{10,9},{11,1... | collective-permute-start | bytes 2211848 | tf_op jit(solution)/shard_map/ppermute | solution.py:16
  165.2 7.8 %slice-start = ((s8[11796480]{0:T(1024)(128)(4,1)}), s8[4194304]{0:T(1024)(128)(4,1)S(1)}, s32[]{:S(2)}) async-start(s8[11796480]{0:T(1024)(128)(4,1)} %bitcast.66), calls=%async_computation.2 | async-start | bytes 8388608
  165.2 7.8 %slice-start.1 = ((s8[11796480]{0:T(1024)(128)(4,1)}), s8[4194304]{0:T(1024)(128)(4,1)S(1)}, s32[]{:S(2)}) async-start(s8[11796480]{0:T(1024)(128)(4,1)} %bitcast.66), calls=%async_computation.3 | async-start | bytes 8388608
  168.4 4.7 %slice-start.2 = ((s8[11796480]{0:T(1024)(128)(4,1)}), s8[3407872]{0:T(1024)(128)(4,1)S(1)}, s32[]{:S(2)}) async-start(s8[11796480]{0:T(1024)(128)(4,1)} %bitcast.66), calls=%async_computation.4 | async-start | bytes 6815744
  177.0 41.0 %copy-start.5 = (bf16[2,1440,256]{2,1,0:T(8,128)(2,1)S(1)}, bf16[2,1440,256]{2,1,0:T(8,128)(2,1)}, u32[]{:S(2)}) copy-start(bf16[2,1440,256]{2,1,0:T(8,128)(2,1)} %copy-done.4) | copy-start | bytes 4423684
  211.7 10.1 %copy-start.3 = (bf16[2,1440,256]{2,1,0:T(8,128)(2,1)S(1)}, bf16[2,1440,256]{2,1,0:T(8,128)(2,1)}, u32[]{:S(2)}) copy-start(bf16[2,1440,256]{2,1,0:T(8,128)(2,1)} %copy-done.2) | copy-start | bytes 4423684
  211.8 5.6 %collective-permute-start.5 = (bf16[64,256]{1,0:T(8,128)(2,1)S(1)}, bf16[64,256]{1,0:T(8,128)(2,1)S(1)}, u32[]{:S(2)}, u32[]{:S(2)}) collective-permute-start(bf16[64,256]{1,0:T(8,128)(2,1)S(1)} %reduce_sum.32), channel_id=1, source_target_pairs={{0,8},{2,10},{4,12},{6,14},{8,0},{10,2},{12,4},{14,6},{1,9},{3,11}... | collective-permute-start | bytes 98312 | tf_op jit(solution)/shard_map/ppermute | solution.py:182
  217.4 4.3 %collective-permute-start.6 = (bf16[2,64,256]{2,1,0:T(8,128)(2,1)S(1)}, bf16[2,64,256]{2,1,0:T(8,128)(2,1)S(1)}, u32[]{:S(2)}, u32[]{:S(2)}) collective-permute-start(bf16[2,64,256]{2,1,0:T(8,128)(2,1)S(1)} %pad_maximum_fusion.3), channel_id=1, source_target_pairs={{0,4},{2,6},{4,0},{6,2},{8,12},{10,14},{12,8},{14,10},{1,5},{3,7},... | collective-permute-start | bytes 196616 | tf_op jit(solution)/shard_map/ppermute | solution.py:182
  221.8 5.0 %collective-permute-start.7 = (bf16[2,2,64,256]{3,2,1,0:T(8,128)(2,1)S(1)}, bf16[2,2,64,256]{3,2,1,0:T(8,128)(2,1)S(1)}, u32[]{:S(2)}, u32[]{:S(2)}) collective-permute-start(bf16[2,2,64,256]{3,2,1,0:T(8,128)(2,1)S(1)} %pad_maximum_fusion.2), channel_id=1, source_target_pairs={{0,2},{2,0},{4,6},{6,4},{8,10},{10,8},{12,14},{14,12},{1,3},{3,1},... | collective-permute-start | bytes 393224 | tf_op jit(solution)/shard_map/ppermute | solution.py:182
